TPU v7x, 256 devices: a whole 4x4x8 slice. The times are simulated.
256 devices in a mesh: dp: 16 (over z_lo, x), tensor: 16 (over y, z_hi, core).
Axes of the slice: x: 4, y: 4, z: 8 (z_hi: 2, z_lo: 4; z = z_hi * 4 + z_lo), core: 2. Of those that a mesh axis runs over, the one named last changes fastest.
Arguments:
- queries: bfloat16 [4096, 6144], P('dp', 'tensor'), may hold values from -28 to 28
- key_rows: bfloat16 [4096, 6144], P('dp', 'tensor'), may hold values from -4 to 4
- value_rows: bfloat16 [4096, 6144], P('dp', 'tensor'), may hold values from -6 to 6
- residual_in: bfloat16 [4096, 12288], P(('dp', 'tensor')), may hold values from -3 to 3
- out_weight: bfloat16 [12288, 6144], P('dp', 'tensor'), may hold values from -0.25 to 0.25
- encoder: bfloat16 [96, 32, 128], replicated, may hold values from -0.5 to 0.5
- decoder: bfloat16 [96, 32, 128], replicated, may hold values from -1 to 1
- grad_out: bfloat16 [4096, 12288], P(('dp', 'tensor')), may hold values from -2.5 to 2.5
Outputs:
- layer_out: bfloat16 [4096, 12288], P('dp')
- grad_queries: bfloat16 [4096, 6144], P('dp', 'tensor')
- grad_keys: bfloat16 [4096, 6144], P('dp', 'tensor')
- grad_values: bfloat16 [4096, 6144], P('dp', 'tensor')
- grad_weight: float32 [12288, 6144], P('dp', 'tensor')
All inputs are finite; a program needn't handle non-finite values.
Results may differ from a plain program's by a relative error of at most 0.022.
Values may be sent and summed in bfloat16 or wider, within the bound.
A program may use at most 128 MiB of HBM per device.

v0:
```python
import math

import jax
import jax.numpy as jnp
from jax import lax
from jax.sharding import PartitionSpec as P

HD = 128


NEG_FILL = -1e30


def split_heads(matrix, head_size):
    return matrix.reshape(matrix.shape[0], matrix.shape[1] // head_size, head_size)


def causal_probs(query_heads, key_heads):
    length = query_heads.shape[0]
    score_scale = 1.0 / math.sqrt(query_heads.shape[2])
    scores = (
        jnp.einsum("qhd,khd->hqk", query_heads, key_heads, preferred_element_type=jnp.float32)
        * score_scale
    )
    row_index = lax.broadcasted_iota(jnp.int32, (length, length), 0)
    col_index = lax.broadcasted_iota(jnp.int32, (length, length), 1)
    scores = jnp.where(col_index <= row_index, scores, NEG_FILL)
    row_max = jnp.max(scores, axis=-1, keepdims=True)
    weights = jnp.exp(scores - row_max)
    return weights / jnp.sum(weights, axis=-1, keepdims=True)


def attend_forward(queries, key_rows, value_rows, head_size):
    probs = causal_probs(split_heads(queries, head_size), split_heads(key_rows, head_size))
    probs_bf = probs.astype(jnp.bfloat16)
    mixed = jnp.einsum(
        "hqk,khd->qhd",
        probs_bf,
        split_heads(value_rows, head_size),
        preferred_element_type=jnp.float32,
    )
    return mixed.astype(jnp.bfloat16).reshape(queries.shape)


def attend_backward(queries, key_rows, value_rows, grad_attn, head_size):
    query_heads = split_heads(queries, head_size)
    key_heads = split_heads(key_rows, head_size)
    value_heads = split_heads(value_rows, head_size)
    grad_heads = split_heads(grad_attn, head_size)
    probs = causal_probs(query_heads, key_heads)
    probs_bf = probs.astype(jnp.bfloat16)
    dprobs = jnp.einsum("qhd,khd->hqk", grad_heads, value_heads, preferred_element_type=jnp.float32)
    center = jnp.sum(dprobs * probs, axis=-1, keepdims=True)
    grad_scores = (probs * (dprobs - center) * (1.0 / math.sqrt(head_size))).astype(jnp.bfloat16)
    grad_query = jnp.einsum(
        "hqk,khd->qhd", grad_scores, key_heads, preferred_element_type=jnp.float32
    )
    grad_key = jnp.einsum(
        "hqk,qhd->khd", grad_scores, query_heads, preferred_element_type=jnp.float32
    )
    grad_value = jnp.einsum(
        "hqk,qhd->khd", probs_bf, grad_heads, preferred_element_type=jnp.float32
    )
    shape = queries.shape
    return (
        grad_query.astype(jnp.bfloat16).reshape(shape),
        grad_key.astype(jnp.bfloat16).reshape(shape),
        grad_value.astype(jnp.bfloat16).reshape(shape),
    )


def encode(partial_value, encoder):
    count = partial_value.shape[0]
    block_count, code_width, block_size = encoder.shape
    blocks = partial_value.reshape(count, block_count, block_size)
    coded = jnp.einsum(
        "nbk,bck->nbc", blocks, encoder.astype(jnp.float32), precision=lax.Precision.HIGHEST
    )
    return coded.reshape(count, block_count * code_width)


def decode(code_sum, decoder):
    count = code_sum.shape[0]
    block_count, code_width, block_size = decoder.shape
    blocks = code_sum.reshape(count, block_count, code_width)
    opened = jnp.einsum(
        "nbc,bck->nbk", blocks, decoder.astype(jnp.float32), precision=lax.Precision.HIGHEST
    )
    return opened.reshape(count, block_count * block_size)


def code_grad(grad_rows, decoder):
    count = grad_rows.shape[0]
    block_count, code_width, block_size = decoder.shape
    blocks = grad_rows.reshape(count, block_count, block_size)
    coded = jnp.einsum("nbk,bck->nbc", blocks, decoder, preferred_element_type=jnp.float32)
    return coded.reshape(count, block_count * code_width).astype(jnp.bfloat16)


def expand(grad_codes, encoder):
    block_count, code_width, block_size = encoder.shape
    count = grad_codes.shape[0]
    blocks = grad_codes.reshape(count, block_count, code_width)
    opened = jnp.einsum("nbc,bck->nbk", blocks, encoder, preferred_element_type=jnp.float32)
    return opened.reshape(count, block_count * block_size).astype(jnp.bfloat16)


def local(queries, key_rows, value_rows, residual_in, out_weight, encoder, decoder, grad_out):
    attn_out = attend_forward(queries, key_rows, value_rows, HD)
    weight_full = lax.all_gather(out_weight, "dp", axis=0, tiled=True)
    partial_value = lax.dot_general(
        attn_out, weight_full, (((1,), (1,)), ((), ())), preferred_element_type=jnp.float32
    )
    code_sum = lax.psum_scatter(
        encode(partial_value, encoder).astype(jnp.bfloat16),
        "tensor",
        scatter_dimension=0,
        tiled=True,
    ).astype(jnp.float32)
    layer_rows = (residual_in.astype(jnp.float32) + decode(code_sum, decoder)).astype(jnp.bfloat16)
    layer_out = lax.all_gather(layer_rows, "tensor", axis=0, tiled=True)
    grad_codes = code_grad(grad_out, decoder)
    piece = lax.all_gather(grad_codes, "tensor", axis=0, tiled=True)
    grad_partial_rows = expand(piece, encoder)
    grad_attn_rows = jnp.dot(
        grad_partial_rows, weight_full, preferred_element_type=jnp.float32
    ).astype(jnp.bfloat16)
    grad_weight = lax.psum_scatter(
        lax.dot_general(
            grad_partial_rows,
            attn_out,
            (((0,), (0,)), ((), ())),
            preferred_element_type=jnp.float32,
        ).astype(jnp.bfloat16),
        "dp",
        scatter_dimension=0,
        tiled=True,
    ).astype(jnp.float32)
    grad_query, grad_key, grad_value = attend_backward(
        queries, key_rows, value_rows, grad_attn_rows, HD
    )
    return (layer_out, grad_query, grad_key, grad_value, grad_weight)


def solution(mesh):
    placed = (
        P("dp", "tensor"),
        P("dp", "tensor"),
        P("dp", "tensor"),
        P(("dp", "tensor"), None),
        P("dp", "tensor"),
        P(),
        P(),
        P(("dp", "tensor"), None),
    )
    return jax.shard_map(
        local,
        mesh=mesh,
        in_specs=placed,
        out_specs=(
            P("dp", None),
            P("dp", "tensor"),
            P("dp", "tensor"),
            P("dp", "tensor"),
            P("dp", "tensor"),
        ),
        check_vma=False,
    )
```

profile of v0, /device:TPU:1, one launch (start us, length us, event | category | flops | bytes accessed | tf_op | source)
XLA Modules:
  0.0 487.5 jit_solution(14030851859615496268)
XLA Ops:
  8.0 1.7 fusion.9
  9.8 1.0 convert_element_type.88
  11.0 1.1 copy.33
  12.0 1.1 copy.29
  13.1 1.1 copy.30
  14.2 1.3 fusion.29
  16.1 110.5 %all-gather.4.cloned.1.call-done = bf16[12288,384]{1,0:T(8,128)(2,1)} async-done(((bf16[768,384]{1,0:T(8,128)(2,1)}), bf16[12288,384]{1,0:T(8,128)(2,1)}) %all-gather.4.cloned.1.call-update) | async-done | bytes 9437200 | tf_op jit(solution)/shard_map/all_gather | solution.py:110
  126.6 12.4 %fusion.30 = f32[256,96,128]{2,0,1:T(8,128)} fusion(bf16[256,384,1]{0,1,2:T(8,128)(2,1)S(1)} %bitcast.71, bf16[96,128,384]{2,1,0:T(8,128)(2,1)} %bitcast.66), kind=kOutput, calls=%fused_computation.43 | convolution fusion | flops 2415919104 | bytes 22216704 | tf_op jit(solution)/shard_map/dot_general | solution.py:111
  139.0 10.1 %convolution_convert_fusion.2 = bf16[96,256,32]{1,2,0:T(8,128)(2,1)S(1)} fusion(f32[256,96,128]{2,0,1:T(8,128)} %fusion.30, bf16[96,32,128]{2,1,0:T(8,128)(2,1)S(1)} %copy-done), kind=kOutput, calls=%fused_computation.4 | convolution fusion | flops 1208745984 | bytes 14942208 | tf_op jit(solution)/shard_map/nbk,bck->nbc/dot_general | solution.py:76
  149.2 1.8 copy.35
  151.2 35.2 %all-gather.8.cloned.1.call-done = bf16[256,3072]{1,0:T(8,128)(2,1)} async-done(((bf16[16,3072]{1,0:T(8,128)(2,1)}), bf16[256,3072]{1,0:T(8,128)(2,1)}) %all-gather.8.cloned.1.call-update) | async-done | bytes 1572880 | tf_op jit(solution)/shard_map/all_gather | solution.py:123
  186.4 1.7 copy.40
  188.1 1.8 convolution_convert_fusion.1
  190.0 2.7 copy-done.2
  192.7 5.8 %convolution_convert_fusion = bf16[12288,384]{1,0:T(8,128)(2,1)} fusion(bf16[256,12288]{0,1:T(8,128)(2,1)S(1)} %bitcast.67, bf16[256,384]{0,1:T(8,128)(2,1)S(1)} %bitcast.72), kind=kOutput, calls=%fused_computation.2 | convolution fusion | flops 2420637696 | bytes 15925248 | tf_op jit(solution)/shard_map/dot_general | solution.py:129
  198.5 69.6 %reduce-scatter.3.cloned.1.call-done = bf16[16,3072]{1,0:T(8,128)(2,1)} async-done(((bf16[256,3072]{1,0:T(8,128)(2,1)}), bf16[16,3072]{1,0:T(8,128)(2,1)}) %reduce-scatter.3.cloned.1.call-update) | async-done | bytes 98320 | tf_op jit(solution)/shard_map/reduce_scatter | solution.py:114
  268.1 1.2 reshape.65
  270.6 9.0 %convolution_convert_fusion.8 = bf16[256,384]{1,0:T(8,128)(2,1)S(1)} fusion(bf16[256,12288]{0,1:T(8,128)(2,1)} %bitcast.68, bf16[12288,384]{1,0:T(8,128)(2,1)} %all-gather.4.cloned.1.call-done), kind=kOutput, calls=%fused_computation.20 | convolution fusion | flops 2416017408 | bytes 15925248 | tf_op jit(solution)/shard_map/dot_general | solution.py:125
  280.1 1.8 convolution_convert_fusion.4
  282.7 1.8 convolution_convert_fusion.7
  286.8 94.9 %reduce-scatter.5.cloned.1.call-done = bf16[768,384]{1,0:T(8,128)(2,1)} async-done(((bf16[12288,384]{1,0:T(8,128)(2,1)}), bf16[768,384]{1,0:T(8,128)(2,1)}) %reduce-scatter.5.cloned.1.call-update) | async-done | bytes 589840 | tf_op jit(solution)/shard_map/reduce_scatter | solution.py:128
  381.7 2.2 convert_element_type.101
  383.9 90.9 %all-gather.6.cloned.1.call-done = bf16[256,12288]{1,0:T(8,128)(2,1)} async-done(((bf16[16,12288]{1,0:T(8,128)(2,1)}), bf16[256,12288]{1,0:T(8,128)(2,1)}) %all-gather.6.cloned.1.call-update) | async-done | bytes 6291472 | tf_op jit(solution)/shard_map/all_gather | solution.py:121
  474.8 6.1 %copy.68 = bf16[256,12288]{1,0:T(8,128)(2,1)} copy(bf16[256,12288]{1,0:T(8,128)(2,1)} %all-gather.6.cloned.1.call-done) | data formatting | bytes 12582912
  (30 shorter events, 6.7 us)
Async XLA Ops:
  7.2 131.9 %copy-start = (bf16[96,32,128]{2,1,0:T(8,128)(2,1)S(1)}, bf16[96,32,128]{2,1,0:T(8,128)(2,1)}, u32[]{:S(2)}) copy-start(bf16[96,32,128]{2,1,0:T(8,128)(2,1)} %param.13) | copy-start | bytes 2359300
  7.2 119.4 %all-gather.4.cloned.1.call-start = ((), (), s32[]{:S(2)}) async-start(), calls=%async_computation.2 | async-start | bytes 10027008 | tf_op jit(solution)/shard_map/all_gather | solution.py:110
  7.9 178.5 %all-gather.8.cloned.1.call-start = ((), (), s32[]{:S(2)}) async-start(), calls=%async_computation.5 | async-start | bytes 1671168 | tf_op jit(solution)/shard_map/all_gather | solution.py:123
  10.9 257.2 %reduce-scatter.3.cloned.1.call-start = ((), (), s32[]{:S(2)}) async-start(), calls=%async_computation.3 | async-start | bytes 1671168 | tf_op jit(solution)/shard_map/reduce_scatter | solution.py:114
  151.0 230.7 %reduce-scatter.5.cloned.1.call-start = ((), (), s32[]{:S(2)}) async-start(), calls=%async_computation.6 | async-start | bytes 10027008 | tf_op jit(solution)/shard_map/reduce_scatter | solution.py:128
  190.0 2.7 copy-start.2
  198.5 70.9 %copy-start.3 = (bf16[96,32,128]{2,1,0:T(8,128)(2,1)S(1)}, bf16[96,32,128]{2,1,0:T(8,128)(2,1)}, u32[]{:S(2)}) copy-start(bf16[96,32,128]{2,1,0:T(8,128)(2,1)} %param.14) | copy-start | bytes 2359300
  198.5 71.2 %copy-start.4 = (bf16[16,12288]{1,0:T(8,128)(2,1)S(1)}, bf16[16,12288]{1,0:T(8,128)(2,1)}, u32[]{:S(2)}) copy-start(bf16[16,12288]{1,0:T(8,128)(2,1)} %param.11) | copy-start | bytes 1179652
  198.5 276.3 %all-gather.6.cloned.1.call-start = ((), (), s32[]{:S(2)}) async-start(), calls=%async_computation.4 | async-start | bytes 6684672 | tf_op jit(solution)/shard_map/all_gather | solution.py:121
  381.7 99.3 %copy-start.1 = (bf16[96,32,128]{2,1,0:T(8,128)(2,1)S(1)}, bf16[96,32,128]{2,1,0:T(8,128)(2,1)}, u32[]{:S(2)}) copy-start(bf16[96,32,128]{2,1,0:T(8,128)(2,1)} %param.13) | copy-start | bytes 2359300
Sparse Core Ops, SparseCore 0:
  9.8 116.7 all-gather.3
  129.9 56.4 all-gather.7
  190.6 77.5 reduce-scatter.2
  270.6 111.0 reduce-scatter.4
  384.2 90.5 all-gather.5
where the time goes:
time: 488 us; the launch traced here: 487 us
  waiting for transfers between devices  402 us (82%)
  matrix products  47.8 us (10%)
  local copies, waits for them, and re-layouts  20.5 us (4%)
  between operations  13.9 us (3%)
    all_gather x1, waiting for transfers between devices, local(): weight_full = lax.all_gather(out_weight, 'dp', axis=0, tiled=True)  110 us
    reduce_scatter x1, waiting for transfers between devices, local(): lax.psum_scatter(lax.dot_general(grad_partial_rows, attn_out, (((0,), (0,...  94.9 us
    all_gather x1, waiting for transfers between devices, local(): layer_out = lax.all_gather(layer_rows, 'tensor', axis=0, tiled=True)  90.9 us
    reduce_scatter x1, waiting for transfers between devices, local(): lax.psum_scatter(encode(partial_value, encoder).astype(jnp.bfloat16), 'te...  69.6 us
    all_gather x1, waiting for transfers between devices, local(): piece = lax.all_gather(grad_codes, 'tensor', axis=0, tiled=True)  35.2 us
    unnamed x17, local copies, waits for them, and re-layouts  14.5 us
    dot_general x1, matrix products, local(): lax.dot_general(attn_out, weight_full, (((1,), (1,)), ((), ())), preferre...  12.4 us
    dot_general x1, matrix products, encode(): jnp.einsum('nbk,bck->nbc', blocks, encoder.astype(jnp.float32), precision...  10.1 us
  transfers between devices with their start and end apart: 5, of which 5 were waited for; matrix products, arithmetic and copies ran while one was open for 13% of the time, Pallas kernels for 0%

commit v1 on v0

--- a/solution.py
+++ b/solution.py
@@ -69,23 +69,17 @@
     )
 
 
-def encode(partial_value, encoder):
-    count = partial_value.shape[0]
-    block_count, code_width, block_size = encoder.shape
-    blocks = partial_value.reshape(count, block_count, block_size)
-    coded = jnp.einsum(
-        "nbk,bck->nbc", blocks, encoder.astype(jnp.float32), precision=lax.Precision.HIGHEST
-    )
-    return coded.reshape(count, block_count * code_width)
+def fold_weight(weight_rows, encoder_rows):
+    blocks = weight_rows.reshape(encoder_rows.shape[0], encoder_rows.shape[2], weight_rows.shape[1])
+    folded = jnp.einsum("bck,bkh->bch", encoder_rows, blocks, preferred_element_type=jnp.float32)
+    return folded.reshape(-1, weight_rows.shape[1]).astype(jnp.bfloat16)
 
 
 def decode(code_sum, decoder):
     count = code_sum.shape[0]
     block_count, code_width, block_size = decoder.shape
     blocks = code_sum.reshape(count, block_count, code_width)
-    opened = jnp.einsum(
-        "nbc,bck->nbk", blocks, decoder.astype(jnp.float32), precision=lax.Precision.HIGHEST
-    )
+    opened = jnp.einsum("nbc,bck->nbk", blocks, decoder, preferred_element_type=jnp.float32)
     return opened.reshape(count, block_count * block_size)
 
 
@@ -97,48 +91,42 @@
     return coded.reshape(count, block_count * code_width).astype(jnp.bfloat16)
 
 
-def expand(grad_codes, encoder):
+def local(queries, key_rows, value_rows, residual_in, out_weight, encoder, decoder, grad_out):
     block_count, code_width, block_size = encoder.shape
-    count = grad_codes.shape[0]
-    blocks = grad_codes.reshape(count, block_count, code_width)
-    opened = jnp.einsum("nbc,bck->nbk", blocks, encoder, preferred_element_type=jnp.float32)
-    return opened.reshape(count, block_count * block_size).astype(jnp.bfloat16)
-
-
-def local(queries, key_rows, value_rows, residual_in, out_weight, encoder, decoder, grad_out):
+    own_blocks = out_weight.shape[0] // block_size
+    encoder_rows = lax.dynamic_slice_in_dim(
+        encoder, lax.axis_index("dp") * own_blocks, own_blocks, 0
+    )
+    folded = lax.all_gather(fold_weight(out_weight, encoder_rows), "dp", axis=0, tiled=True)
+    grad_codes = lax.all_gather(code_grad(grad_out, decoder), "tensor", axis=0, tiled=True)
+    residual = lax.all_gather(residual_in, "tensor", axis=0, tiled=True)
     attn_out = attend_forward(queries, key_rows, value_rows, HD)
-    weight_full = lax.all_gather(out_weight, "dp", axis=0, tiled=True)
-    partial_value = lax.dot_general(
-        attn_out, weight_full, (((1,), (1,)), ((), ())), preferred_element_type=jnp.float32
+    codes = lax.dot_general(
+        attn_out, folded, (((1,), (1,)), ((), ())), preferred_element_type=jnp.float32
+    ).astype(jnp.bfloat16)
+    code_rows = lax.psum_scatter(codes, "tensor", scatter_dimension=0, tiled=True)
+    code_sum = lax.all_gather(code_rows, "tensor", axis=0, tiled=True)
+    grad_attn_rows = jnp.dot(grad_codes, folded, preferred_element_type=jnp.float32).astype(
+        jnp.bfloat16
     )
-    code_sum = lax.psum_scatter(
-        encode(partial_value, encoder).astype(jnp.bfloat16),
-        "tensor",
-        scatter_dimension=0,
-        tiled=True,
-    ).astype(jnp.float32)
-    layer_rows = (residual_in.astype(jnp.float32) + decode(code_sum, decoder)).astype(jnp.bfloat16)
-    layer_out = lax.all_gather(layer_rows, "tensor", axis=0, tiled=True)
-    grad_codes = code_grad(grad_out, decoder)
-    piece = lax.all_gather(grad_codes, "tensor", axis=0, tiled=True)
-    grad_partial_rows = expand(piece, encoder)
-    grad_attn_rows = jnp.dot(
-        grad_partial_rows, weight_full, preferred_element_type=jnp.float32
-    ).astype(jnp.bfloat16)
-    grad_weight = lax.psum_scatter(
+    code_weight = lax.psum_scatter(
         lax.dot_general(
-            grad_partial_rows,
-            attn_out,
-            (((0,), (0,)), ((), ())),
-            preferred_element_type=jnp.float32,
+            grad_codes, attn_out, (((0,), (0,)), ((), ())), preferred_element_type=jnp.float32
         ).astype(jnp.bfloat16),
         "dp",
         scatter_dimension=0,
         tiled=True,
-    ).astype(jnp.float32)
+    )
+    grad_weight = jnp.einsum(
+        "bck,bch->bkh",
+        encoder_rows,
+        code_weight.reshape(own_blocks, code_width, -1),
+        preferred_element_type=jnp.float32,
+    ).reshape(out_weight.shape)
     grad_query, grad_key, grad_value = attend_backward(
         queries, key_rows, value_rows, grad_attn_rows, HD
     )
+    layer_out = (residual.astype(jnp.float32) + decode(code_sum, decoder)).astype(jnp.bfloat16)
     return (layer_out, grad_query, grad_key, grad_value, grad_weight)
 
 

time: 488 us -> 498 us (1.020)
  waiting for transfers between devices: 402 us -> 425 us
  matrix products: 47.8 us -> 29.1 us
  other arithmetic: 3.12 us -> 10.7 us
    all_gather x3 -> x4, waiting for transfers between devices: 237 us -> 277 us  [the longest x1 74.5 us: local(): lax.all_gather(fold_weight(out_weight, encoder_rows), 'dp', axis=0, tiled...]
    dot_general x6, matrix products: 39.5 us -> 21 us  [the longest x1 6.31 us: decode(): jnp.einsum('nbc,bck->nbk', blocks, decoder, preferred_element_type=jnp.fl...]
    reduce_scatter x2, waiting for transfers between devices: 164 us -> 147 us  [the longest x1 77.8 us: local(): lax.psum_scatter(codes, 'tensor', scatter_dimension=0, tiled=True)]
    unnamed x17 -> x16, local copies, waits for them, and re-layouts: 14.5 us -> 2.92 us
    reshape x1, local copies, waits for them, and re-layouts: 1.19 us -> 12.7 us  [decode(): return opened.reshape(count, block_count * block_size)]
    convert_element_type x2 -> x1, other arithmetic: 3.09 us -> 10.7 us  [local(): (residual.astype(jnp.float32) + decode(code_sum, decoder)).astype(jnp.bfl...]
  transfers between devices with their start and end apart: 5 -> 6, of which waited for: 5 -> 6; matrix products, arithmetic and copies ran while one was open for 13% -> 9% of each run, Pallas kernels for 0% -> 0%
where the time goes in v1:
time: 498 us
  waiting for transfers between devices  425 us (85%)
  matrix products  29.1 us (6%)
  local copies, waits for them, and re-layouts  18.6 us (4%)
  between operations  14.3 us (3%)
  other arithmetic  10.7 us (2%)
    reduce_scatter x1, waiting for transfers between devices, local(): lax.psum_scatter(codes, 'tensor', scatter_dimension=0, tiled=True)  77.8 us
    all_gather x1, waiting for transfers between devices, local(): lax.all_gather(fold_weight(out_weight, encoder_rows), 'dp', axis=0, tiled...  74.5 us
    all_gather x1, waiting for transfers between devices, local(): residual = lax.all_gather(residual_in, 'tensor', axis=0, tiled=True)  70.8 us
    reduce_scatter x1, waiting for transfers between devices, local(): lax.psum_scatter(lax.dot_general(grad_codes, attn_out, (((0,), (0,)), (()...  68.9 us
    all_gather x1, waiting for transfers between devices, local(): code_sum = lax.all_gather(code_rows, 'tensor', axis=0, tiled=True)  66.1 us
    all_gather x1, waiting for transfers between devices, local(): lax.all_gather(code_grad(grad_out, decoder), 'tensor', axis=0, tiled=True)  66 us
    reshape x1, local copies, waits for them, and re-layouts, decode(): return opened.reshape(count, block_count * block_size)  12.7 us
    convert_element_type x1, other arithmetic, local(): (residual.astype(jnp.float32) + decode(code_sum, decoder)).astype(jnp.bfl...  10.7 us
  transfers between devices with their start and end apart: 6, of which 6 were waited for; matrix products, arithmetic and copies ran while one was open for 9% of the time, Pallas kernels for 0%

profile of v1, /device:TPU:1, one launch (start us, length us, event | category | flops | bytes accessed | tf_op | source)
XLA Modules:
  0.0 497.6 jit_solution(11995187900959077663)
XLA Ops:
  7.3 2.1 convolution_convert_fusion.8
  9.4 1.5 fusion.9
  11.1 1.0 convert_element_type.71
  12.7 1.3 fusion.32
  14.6 74.5 %all-gather.7.cloned.1.call-done = bf16[3072,384]{1,0:T(8,128)(2,1)} async-done(((bf16[192,384]{1,0:T(8,128)(2,1)}), bf16[3072,384]{1,0:T(8,128)(2,1)}) %all-gather.7.cloned.1.call-update) | async-done | bytes 2359312 | tf_op jit(solution)/shard_map/all_gather | solution.py:100
  89.1 3.8 convolution_convert_fusion.1
  93.1 66.0 %all-gather.11.cloned.1.call-done = bf16[256,3072]{1,0:T(8,128)(2,1)} async-done(((bf16[16,3072]{1,0:T(8,128)(2,1)}), bf16[256,3072]{1,0:T(8,128)(2,1)}) %all-gather.11.cloned.1.call-update) | async-done | bytes 1572880 | tf_op jit(solution)/shard_map/all_gather | solution.py:101
  159.1 3.8 convolution_convert_fusion
  163.0 77.8 %reduce-scatter.3.cloned.1.call-done = bf16[16,3072]{1,0:T(8,128)(2,1)} async-done(((bf16[256,3072]{1,0:T(8,128)(2,1)}), bf16[16,3072]{1,0:T(8,128)(2,1)}) %reduce-scatter.3.cloned.1.call-update) | async-done | bytes 98320 | tf_op jit(solution)/shard_map/reduce_scatter | solution.py:107
  241.4 2.6 convolution_convert_fusion.3
  244.5 1.8 convolution_convert_fusion.4
  246.3 0.8 copy.47
  247.2 1.8 convolution_convert_fusion.7
  249.0 0.8 copy.48
  249.8 0.6 convolution_convert_fusion.6
  250.5 0.8 copy.49
  251.3 68.9 %reduce-scatter.5.cloned.1.call-done = bf16[192,384]{1,0:T(8,128)(2,1)} async-done(((bf16[3072,384]{1,0:T(8,128)(2,1)}), bf16[192,384]{1,0:T(8,128)(2,1)}) %reduce-scatter.5.cloned.1.call-update) | async-done | bytes 147472 | tf_op jit(solution)/shard_map/reduce_scatter | solution.py:112
  320.2 2.3 fusion.20
  322.5 66.1 %all-gather.9.cloned.1.call-done = bf16[256,3072]{1,0:T(8,128)(2,1)} async-done(((bf16[16,3072]{1,0:T(8,128)(2,1)}), bf16[256,3072]{1,0:T(8,128)(2,1)}) %all-gather.9.cloned.1.call-update) | async-done | bytes 1572880 | tf_op jit(solution)/shard_map/all_gather | solution.py:108
  388.6 1.7 copy.37
  390.3 6.3 %fusion.33 = f32[96,256,128]{1,2,0:T(8,128)} fusion(bf16[256,96,32]{0,2,1:T(8,128)(2,1)S(1)} %bitcast.57, bf16[96,32,128]{2,1,0:T(8,128)(2,1)S(1)} %copy-done), kind=kOutput, calls=%fused_computation.45 | convolution fusion | flops 201326592 | bytes 14942208 | tf_op jit(solution)/shard_map/nbc,bck->nbk/dot_general | solution.py:82
  396.7 12.7 %copy.38 = f32[256,12288]{1,0:T(8,128)} copy(f32[256,12288]{0,1:T(8,128)} %bitcast.56) | data formatting | bytes 25165824 | tf_op jit(solution)/shard_map/reshape | solution.py:83
  409.3 70.8 %all-gather.5.cloned.1.call-done = bf16[256,12288]{1,0:T(8,128)(2,1)} async-done(((bf16[16,12288]{1,0:T(8,128)(2,1)}), bf16[256,12288]{1,0:T(8,128)(2,1)}) %all-gather.5.cloned.1.call-update) | async-done | bytes 6291472 | tf_op jit(solution)/shard_map/all_gather | solution.py:102
  480.1 10.7 %add_convert_fusion = bf16[256,12288]{1,0:T(8,128)(2,1)} fusion(f32[256,12288]{1,0:T(8,128)} %copy.38, bf16[256,12288]{1,0:T(8,128)(2,1)} %all-gather.5.cloned.1.call-done), kind=kLoop, calls=%fused_computation.2 | loop fusion | flops 9437184 | bytes 25165824 | tf_op jit(solution)/shard_map/convert_element_type | solution.py:129
  (30 shorter events, 2.5 us)
Async XLA Ops:
  7.2 2.2 copy-start
  7.2 5.0 %copy-start.2 = (bf16[256,384]{1,0:T(8,128)(2,1)S(1)}, bf16[256,384]{1,0:T(8,128)(2,1)}, u32[]{:S(2)}) copy-start(bf16[256,384]{1,0:T(8,128)(2,1)} %param.10) | copy-start | bytes 589828
  7.2 5.1 %copy-start.3 = (bf16[256,384]{1,0:T(8,128)(2,1)S(1)}, bf16[256,384]{1,0:T(8,128)(2,1)}, u32[]{:S(2)}) copy-start(bf16[256,384]{1,0:T(8,128)(2,1)} %param.8) | copy-start | bytes 589828
  7.2 5.3 %copy-start.4 = (bf16[256,384]{1,0:T(8,128)(2,1)S(1)}, bf16[256,384]{1,0:T(8,128)(2,1)}, u32[]{:S(2)}) copy-start(bf16[256,384]{1,0:T(8,128)(2,1)} %param.9) | copy-start | bytes 589828
  7.2 81.9 %all-gather.7.cloned.1.call-start = ((), (), s32[]{:S(2)}) async-start(), calls=%async_computation.3 | async-start | bytes 2506752 | tf_op jit(solution)/shard_map/all_gather | solution.py:100
  9.4 149.7 %all-gather.11.cloned.1.call-start = ((), (), s32[]{:S(2)}) async-start(), calls=%async_computation.6 | async-start | bytes 1671168 | tf_op jit(solution)/shard_map/all_gather | solution.py:101
  12.1 228.7 %reduce-scatter.3.cloned.1.call-start = ((), (), s32[]{:S(2)}) async-start(), calls=%async_computation.4 | async-start | bytes 1671168 | tf_op jit(solution)/shard_map/reduce_scatter | solution.py:107
  93.0 227.2 %reduce-scatter.5.cloned.1.call-start = ((), (), s32[]{:S(2)}) async-start(), calls=%async_computation.7 | async-start | bytes 2506752 | tf_op jit(solution)/shard_map/reduce_scatter | solution.py:112
  162.9 78.5 %copy-start.1 = (bf16[256,3072]{1,0:T(8,128)(2,1)S(1)}, bf16[256,3072]{1,0:T(8,128)(2,1)}, u32[]{:S(2)}) copy-start(bf16[256,3072]{1,0:T(8,128)(2,1)} %all-gather.11.cloned.1.call-done) | copy-start | bytes 4718596
  163.0 225.7 %all-gather.9.cloned.1.call-start = ((), (), s32[]{:S(2)}) async-start(), calls=%async_computation.5 | async-start | bytes 1671168 | tf_op jit(solution)/shard_map/all_gather | solution.py:108
  240.8 239.2 %all-gather.5.cloned.1.call-start = ((), (), s32[]{:S(2)}) async-start(), calls=%async_computation.2 | async-start | bytes 6684672 | tf_op jit(solution)/shard_map/all_gather | solution.py:102
Sparse Core Ops, SparseCore 0:
  10.4 78.6 all-gather.6
  92.4 66.6 all-gather.10
  163.2 77.5 reduce-scatter.2
  243.8 76.3 reduce-scatter.4
  322.8 65.8 all-gather.8
  391.2 88.8 all-gather.4

commit v2 on v1

v2 whole, which is shorter than its diff:
```python
import math

import jax
import jax.numpy as jnp
from jax import lax
from jax.experimental import pallas as pl
from jax.experimental.pallas import tpu as pltpu
from jax.sharding import PartitionSpec as P

HD = 128
NEG_FILL = -1e30
MESH = pl.DeviceIdType.MESH
BF, F32 = jnp.bfloat16, jnp.float32

NX, NZL, NY, NZH, NC = 4, 4, 4, 2, 2
TB = 16
SEQ = 256
HEADS = 3
AW = HEADS * HD
NBLK, CODE_W, BLOCK = 96, 32, 128
CODE = NBLK * CODE_W
D = NBLK * BLOCK
OWN = 6
ER = OWN * CODE_W
CH = NX * ER
HALF = SEQ // NC
PAIR = TB * NZH


def nt(a, b):
    return lax.dot_general(a, b, (((1,), (1,)), ((), ())), preferred_element_type=F32)


def nn(a, b):
    return lax.dot_general(a, b, (((1,), (0,)), ((), ())), preferred_element_type=F32)


def tn(a, b):
    return lax.dot_general(a, b, (((0,), (0,)), ((), ())), preferred_element_type=F32)


def place(t):
    return ((t % NC) * NY + t // (NC * NZH)) * NZH + (t // NC) % NZH


class Sems:
    def __init__(self, send, recv):
        self.send, self.recv, self.used, self.started = send, recv, 0, []

    def copy(self, src, dst, target):
        i = self.used
        self.used += 1
        made = pltpu.make_async_remote_copy(
            src_ref=src,
            dst_ref=dst,
            send_sem=self.send.at[i],
            recv_sem=self.recv.at[i],
            device_id=target,
            device_id_type=MESH,
        )
        made.start()
        self.started.append(made)
        return made


N_SEMS = 160


def main_kernel(
    q_ref, k_ref, v_ref, res_ref, w_ref, enc_ref, dec_ref, go_ref,
    resid_ref, cs_ref, dq_ref, dk_ref, dv_ref, gw_ref,
    ew, gcb, attn_p, probs, ga, enc,
    c_own, c_send, c_recv, y_sum, y_recv, z_sum, z_recv, ag,
    gp, gx_recv, gx_sum, gz_recv,
    send_sem, recv_sem, local_sem,
):
    dp, t = lax.axis_index("dp"), lax.axis_index("tensor")
    zl, x = dp // NX, dp % NX
    y, zh, c = t // (NZH * NC), (t // NC) % NZH, t % NC

    def to_x(k):
        return (zl * NX + (x + k) % NX, t)

    def to_zl(k):
        return (((zl + k) % NZL) * NX + x, t)

    def to_y(k):
        return (dp, (((y + k) % NY) * NZH + zh) * NC + c)

    to_zh = (dp, (y * NZH + 1 - zh) * NC + c)
    to_c = (dp, (y * NZH + zh) * NC + 1 - c)
    steps = (1, 3, 2)

    sems = Sems(send_sem, recv_sem)
    send = sems.copy

    barrier = pltpu.get_barrier_semaphore()
    peers = [to_x(k) for k in steps] + [to_zl(k) for k in steps]
    peers += [to_y(k) for k in steps] + [to_zh, to_c]
    for peer in peers:
        pl.semaphore_signal(barrier, inc=1, device_id=peer, device_id_type=MESH)

    enc_copy = pltpu.make_async_copy(
        enc_ref.at[pl.ds(dp * OWN, OWN)], enc, local_sem.at[0]
    )
    enc_copy.start()
    own_rows = pl.ds(pl.multiple_of(t * TB, TB), TB)
    own_res = pltpu.make_async_copy(res_ref, resid_ref.at[own_rows], local_sem.at[1])
    own_res.start()

    enc_copy.wait()
    for b in range(OWN):
        rows = pl.ds(pl.multiple_of(x * ER + b * CODE_W, CODE_W), CODE_W)
        ew[zl, rows, :] = nn(enc[b], w_ref[b * BLOCK : (b + 1) * BLOCK, :]).astype(BF)

    def place_of(y_, zh_, c_):
        return (c_ * NY + y_) * NZH + zh_

    def block_rows(p, n=1):
        return pl.ds(pl.multiple_of(p * TB, TB), TB * n)

    mine = block_rows(place_of(y, zh, c))
    lane_block = lax.broadcasted_iota(jnp.int32, (TB, BLOCK), 1) // CODE_W
    for g in range(NBLK // 4):
        wide = jnp.concatenate(
            [go_ref[:, (4 * g + j) * BLOCK : (4 * g + j + 1) * BLOCK] for j in range(4)], axis=0
        )
        coded = nt(wide, dec_ref[g * BLOCK : (g + 1) * BLOCK, :])
        picked = coded[:TB]
        for j in range(1, 4):
            picked = jnp.where(lane_block == j, coded[j * TB : (j + 1) * TB], picked)
        gcb[g // 6, mine, (g % 6) * BLOCK : (g % 6 + 1) * BLOCK] = picked.astype(BF)

    pl.semaphore_wait(barrier, len(peers))

    def ew_at(zl_, x_):
        return ew.at[zl_, pl.ds(pl.multiple_of(x_ * ER, ER), ER)]

    gc_z = send(gcb.at[:, mine], gcb.at[:, mine], to_zh)
    gc_y = {}
    for k in steps:
        gc_y[k, 0] = send(gcb.at[:, mine], gcb.at[:, mine], to_y(k))
    ew_z = {k: send(ew_at(zl, x), ew_at(zl, x), to_zl(k)) for k in steps}
    ew_x = {}
    for k in steps:
        ew_x[0, k] = send(ew_at(zl, x), ew_at(zl, x), to_x(k))

    row_index = lax.broadcasted_iota(jnp.int32, (SEQ, SEQ), 0)
    col_index = lax.broadcasted_iota(jnp.int32, (SEQ, SEQ), 1)
    scale = 1.0 / math.sqrt(HD)
    for h in range(HEADS):
        cols = slice(h * HD, (h + 1) * HD)
        scores = nt(q_ref[:, cols], k_ref[:, cols]) * scale
        scores = jnp.where(col_index <= row_index, scores, NEG_FILL)
        weights = jnp.exp(scores - jnp.max(scores, axis=-1, keepdims=True))
        prob = weights / jnp.sum(weights, axis=-1, keepdims=True)
        probs[h] = prob
        mixed = nn(prob.astype(BF), v_ref[:, cols]).astype(BF)
        for b in range(SEQ // TB):
            p = place(b)
            attn_p[p * TB : (p + 1) * TB, cols] = mixed[b * TB : (b + 1) * TB]

    gc_z.wait_recv()
    other = block_rows(place_of(y, 1 - zh, c))
    for k in steps:
        gc_y[k, 1] = send(gcb.at[:, other], gcb.at[:, other], to_y(k))
    pair = block_rows(place_of(y, 0, c), NZH)
    gc_c = [send(gcb.at[:, pair], gcb.at[:, pair], to_c)]
    order = (0,) + steps
    for k in steps:
        ew_z[k].wait_recv()
        from_zl = (zl - k + NZL) % NZL
        for j in steps:
            ew_x[k, j] = send(ew_at(from_zl, x), ew_at(from_zl, x), to_x(j))
    for k in steps:
        gc_y[k, 0].wait_recv()
        gc_y[k, 1].wait_recv()
        pair = block_rows(place_of((y - k + NY) % NY, 0, c), NZH)
        gc_c.append(send(gcb.at[:, pair], gcb.at[:, pair], to_c))
    for made in gc_c:
        made.wait_recv()

    def res_at(y_, zh_):
        return resid_ref.at[pl.ds(pl.multiple_of((y_ * NZH + zh_) * (NC * TB) + c * TB, TB), TB)]

    res_z = send(res_ref, res_at(y, zh), to_zh)
    res_y = {}
    for k in steps:
        res_y[k, 0] = send(res_ref, res_at(y, zh), to_y(k))

    for z_ in range(NZL):
        term = tn(gcb[z_], attn_p[...])
        for x_ in range(NX):
            gp[x_, z_] = term[x_ * ER : (x_ + 1) * ER].astype(BF)
    gx = {}
    for k in steps:
        gx[k] = send(gp.at[(x + k) % NX], gx_recv.at[k - 1], to_x(k))

    zls = [(zl - k + NZL) % NZL for k in order]
    c_cp, y_cp, z_cp, a_cp, ac_cp = {}, {}, {}, {}, {}

    def stage_code(i):
        k, z_ = order[i], zls[i]
        for j in steps:
            ew_x[k, j].wait_recv()
        codes = nt(attn_p[...], ew[z_]).astype(BF)
        for half in range(NC):
            part = codes[half * HALF : (half + 1) * HALF]

            @pl.when(c == half)
            def _():
                c_own[i] = part

            @pl.when(c != half)
            def _():
                c_send[i] = part

        c_cp[i] = send(c_send.at[i], c_recv.at[i], to_c)
        grown = nn(gcb[z_], ew[z_])
        if i == 0:
            ga[...] = grown
        else:
            ga[...] += grown

    def stage_core(i):
        c_cp[i].wait_recv()
        y_sum[i] = (c_own[i].astype(F32) + c_recv[i].astype(F32)).astype(BF)
        for k in steps:
            rows = pl.ds(pl.multiple_of(((y + k) % NY) * PAIR, PAIR), PAIR)
            y_cp[i, k] = send(y_sum.at[i, rows], y_recv.at[i, k - 1], to_y(k))

    def stage_y(i):
        for k in steps:
            y_cp[i, k].wait_recv()
        rows = pl.ds(pl.multiple_of(y * PAIR, PAIR), PAIR)
        total = y_sum[i, rows].astype(F32)
        for k in range(3):
            total += y_recv[i, k].astype(F32)
        z_sum[i] = total.astype(BF)
        z_cp[i] = send(z_sum.at[i], z_recv.at[i], to_zh)

    def ag_rows(y_):
        return pl.ds(pl.multiple_of((c * NY + y_) * PAIR, PAIR), PAIR)

    def stage_z(i):
        z_cp[i].wait_recv()
        z_ = zls[i]
        rows = ag_rows(y)
        ag[z_, rows] = (z_sum[i].astype(F32) + z_recv[i].astype(F32)).astype(BF)
        for k in steps:
            a_cp[i, k] = send(ag.at[z_, rows], ag.at[z_, rows], to_y(k))
        ac_cp[i, 0] = send(ag.at[z_, rows], ag.at[z_, rows], to_c)

    def stage_out(i):
        z_ = zls[i]
        for k in steps:
            a_cp[i, k].wait_recv()
            rows = ag_rows((y - k + NY) % NY)
            ac_cp[i, k] = send(ag.at[z_, rows], ag.at[z_, rows], to_c)

    def stage_done(i):
        for k in order:
            ac_cp[i, k].wait_recv()
        copy = pltpu.make_async_copy(ag.at[zls[i]], cs_ref.at[zls[i]], local_sem.at[2 + i])
        copy.start()
        return copy

    def attention_backward():
        for h in range(HEADS):
            cols = slice(h * HD, (h + 1) * HD)
            grad = jnp.concatenate(
                [ga[place(b) * TB : (place(b) + 1) * TB, cols] for b in range(SEQ // TB)], axis=0
            ).astype(BF)
            prob = probs[h]
            dprobs = nt(grad, v_ref[:, cols])
            center = jnp.sum(dprobs * prob, axis=-1, keepdims=True)
            grad_scores = (prob * (dprobs - center) * scale).astype(BF)
            dq_ref[:, cols] = nn(grad_scores, k_ref[:, cols]).astype(BF)
            dk_ref[:, cols] = tn(grad_scores, q_ref[:, cols]).astype(BF)
            dv_ref[:, cols] = tn(prob.astype(BF), grad).astype(BF)

    stage_code(0)
    stage_core(0)
    res_z.wait_recv()
    for k in steps:
        res_y[k, 1] = send(res_at(y, 1 - zh), res_at(y, 1 - zh), to_y(k))
    res_c = [send(res_ref, res_at(y, zh), to_c)]
    res_c.append(send(res_at(y, 1 - zh), res_at(y, 1 - zh), to_c))
    stage_code(1)
    stage_core(1)
    stage_y(0)
    stage_code(2)
    stage_z(0)
    stage_core(2)
    stage_y(1)
    stage_code(3)
    stage_z(1)
    stage_core(3)
    stage_y(2)
    stage_z(2)
    stage_y(3)
    stage_out(0)
    stage_out(1)
    attention_backward()
    stage_z(3)
    stage_out(2)
    outs = [stage_done(0), stage_done(1)]

    for k in steps:
        gx[k].wait_recv()
    for z_ in range(NZL):
        total = gp[x, z_].astype(F32)
        for k in range(3):
            total += gx_recv[k, z_].astype(F32)
        gx_sum[z_] = total.astype(BF)
    gz = {k: send(gx_sum.at[(zl + k) % NZL], gz_recv.at[k - 1], to_zl(k)) for k in steps}

    stage_out(3)
    outs += [stage_done(2), stage_done(3)]
    for k in steps:
        for zh_ in (0, 1):
            res_y[k, zh_].wait_recv()
            from_zh = zh if zh_ == 0 else 1 - zh
            at = res_at((y - k + NY) % NY, from_zh)
            res_c.append(send(at, at, to_c))

    for k in steps:
        gz[k].wait_recv()
    total = gx_sum[zl].astype(F32)
    for k in range(3):
        total += gz_recv[k].astype(F32)
    summed = total.astype(BF)
    for b in range(OWN):
        gw_ref[b * BLOCK : (b + 1) * BLOCK, :] = tn(
            enc[b], summed[b * CODE_W : (b + 1) * CODE_W]
        )

    for made in res_c:
        made.wait_recv()
    for copy in outs:
        copy.wait()
    own_res.wait()
    for made in sems.started:
        made.wait_send()


STEP_BLOCKS = 8


def close_kernel(
    resid_ref, cs_ref, dec_ref, dq_in, dk_in, dv_in, gw_in,
    out_ref, dq_ref, dk_ref, dv_ref, gw_ref, copy_sem,
):
    step = pl.program_id(0)
    copies = [
        pltpu.make_async_copy(src, dst, copy_sem.at[i])
        for i, (src, dst) in enumerate(
            ((dq_in, dq_ref), (dk_in, dk_ref), (dv_in, dv_ref), (gw_in, gw_ref))
        )
    ]

    @pl.when(step == 0)
    def _():
        for copy in copies:
            copy.start()

    depth, width = STEP_BLOCKS * CODE_W, STEP_BLOCKS * BLOCK
    row = lax.broadcasted_iota(jnp.int32, (depth, BLOCK), 0) // CODE_W
    dec = dec_ref[...]
    opened = jnp.concatenate(
        [jnp.where(row == b, dec, jnp.zeros_like(dec)) for b in range(STEP_BLOCKS)], axis=1
    )
    added = nn(cs_ref[0], opened)
    for b in range(SEQ // TB):
        p = place(b)
        out_ref[b * TB : (b + 1) * TB, :] = (
            resid_ref[b * TB : (b + 1) * TB, :].astype(F32) + added[p * TB : (p + 1) * TB]
        ).astype(BF)

    @pl.when(step == pl.num_programs(0) - 1)
    def _():
        for copy in copies:
            copy.wait()


def local(queries, key_rows, value_rows, residual_in, out_weight, encoder, decoder, grad_out):
    vmem = pl.BlockSpec(memory_space=pltpu.VMEM)
    anywhere = pl.BlockSpec(memory_space=pl.ANY)
    dec_rows = decoder.reshape(CODE, BLOCK)
    resid, code_sum, dq, dk, dv, gw = pl.pallas_call(
        main_kernel,
        out_shape=(
            jax.ShapeDtypeStruct((SEQ, D), BF),
            jax.ShapeDtypeStruct((NZL, SEQ, CH), BF),
            jax.ShapeDtypeStruct((SEQ, AW), BF),
            jax.ShapeDtypeStruct((SEQ, AW), BF),
            jax.ShapeDtypeStruct((SEQ, AW), BF),
            jax.ShapeDtypeStruct((OWN * BLOCK, AW), F32),
        ),
        in_specs=[vmem, vmem, vmem, anywhere, vmem, anywhere, vmem, vmem],
        out_specs=(anywhere, anywhere, vmem, vmem, vmem, vmem),
        scratch_shapes=[
            pltpu.VMEM((NZL, CH, AW), BF),
            pltpu.VMEM((NZL, SEQ, CH), BF),
            pltpu.VMEM((SEQ, AW), BF),
            pltpu.VMEM((HEADS, SEQ, SEQ), F32),
            pltpu.VMEM((SEQ, AW), F32),
            pltpu.VMEM((OWN, CODE_W, BLOCK), BF),
            pltpu.VMEM((4, HALF, CH), BF),
            pltpu.VMEM((4, HALF, CH), BF),
            pltpu.VMEM((4, HALF, CH), BF),
            pltpu.VMEM((4, HALF, CH), BF),
            pltpu.VMEM((4, 3, PAIR, CH), BF),
            pltpu.VMEM((4, PAIR, CH), BF),
            pltpu.VMEM((4, PAIR, CH), BF),
            pltpu.VMEM((NZL, SEQ, CH), BF),
            pltpu.VMEM((NX, NZL, ER, AW), BF),
            pltpu.VMEM((3, NZL, ER, AW), BF),
            pltpu.VMEM((NZL, ER, AW), BF),
            pltpu.VMEM((3, ER, AW), BF),
            pltpu.SemaphoreType.DMA((N_SEMS,)),
            pltpu.SemaphoreType.DMA((N_SEMS,)),
            pltpu.SemaphoreType.DMA((8,)),
        ],
        name="exchange",
        compiler_params=pltpu.CompilerParams(
            collective_id=0, has_side_effects=True, vmem_limit_bytes=48 * 2**20
        ),
    )(queries, key_rows, value_rows, residual_in, out_weight, encoder, dec_rows, grad_out)

    steps = NBLK // STEP_BLOCKS
    per = steps // NZL
    layer_out, dq, dk, dv, gw = pl.pallas_call(
        close_kernel,
        grid=(steps,),
        out_shape=(
            jax.ShapeDtypeStruct((SEQ, D), BF),
            jax.ShapeDtypeStruct((SEQ, AW), BF),
            jax.ShapeDtypeStruct((SEQ, AW), BF),
            jax.ShapeDtypeStruct((SEQ, AW), BF),
            jax.ShapeDtypeStruct((OWN * BLOCK, AW), F32),
        ),
        in_specs=[
            pl.BlockSpec((SEQ, STEP_BLOCKS * BLOCK), lambda i: (0, i)),
            pl.BlockSpec((1, SEQ, STEP_BLOCKS * CODE_W), lambda i: (i // per, 0, i % per)),
            pl.BlockSpec((STEP_BLOCKS * CODE_W, BLOCK), lambda i: (i, 0)),
            anywhere,
            anywhere,
            anywhere,
            anywhere,
        ],
        out_specs=(
            pl.BlockSpec((SEQ, STEP_BLOCKS * BLOCK), lambda i: (0, i)),
            anywhere,
            anywhere,
            anywhere,
            anywhere,
        ),
        scratch_shapes=[pltpu.SemaphoreType.DMA((4,))],
        name="close",
        compiler_params=pltpu.CompilerParams(vmem_limit_bytes=32 * 2**20),
    )(resid, code_sum, dec_rows, dq, dk, dv, gw)
    return layer_out, dq, dk, dv, gw


def solution(mesh):
    placed = (
        P("dp", "tensor"),
        P("dp", "tensor"),
        P("dp", "tensor"),
        P(("dp", "tensor"), None),
        P("dp", "tensor"),
        P(),
        P(),
        P(("dp", "tensor"), None),
    )
    return jax.shard_map(
        local,
        mesh=mesh,
        in_specs=placed,
        out_specs=(
            P("dp", None),
            P("dp", "tensor"),
            P("dp", "tensor"),
            P("dp", "tensor"),
            P("dp", "tensor"),
        ),
        check_vma=False,
    )
```

time: 498 us -> 123 us (0.25)
  waiting for transfers between devices: 425 us -> 0 us
  Pallas kernels: 0 us -> 110 us
  matrix products: 29.1 us -> 0 us
  between operations: 14.3 us -> 0.67 us
  other arithmetic: 10.7 us -> 0 us
  local copies, waits for them, and re-layouts: 18.6 us -> 12.3 us
    all_gather x4 -> x0, waiting for transfers between devices: 277 us -> none  [the longest x1 74.5 us: local(): lax.all_gather(fold_weight(out_weight, encoder_rows), 'dp', axis=0, tiled...]
    reduce_scatter x2 -> x0, waiting for transfers between devices: 147 us -> none  [the longest x1 77.8 us: local(): lax.psum_scatter(codes, 'tensor', scatter_dimension=0, tiled=True)]
    pallas_call x0 -> x2, Pallas kernels: none -> 110 us  [the longest x1 102 us: local(): pl.pallas_call(main_kernel, out_shape=(jax.ShapeDtypeStruct((SEQ, D), BF)...]
    dot_general x12 -> x0, matrix products: 27.7 us -> none  [the longest x1 6.31 us: decode(): jnp.einsum('nbc,bck->nbk', blocks, decoder, preferred_element_type=jnp.fl...]
    reshape x1 -> x0, local copies, waits for them, and re-layouts: 12.7 us -> none  [decode(): return opened.reshape(count, block_count * block_size)]
    convert_element_type x1 -> x0, other arithmetic: 10.7 us -> none  [local(): (residual.astype(jnp.float32) + decode(code_sum, decoder)).astype(jnp.bfl...]
    unnamed x16 -> x20, local copies, waits for them, and re-layouts: 2.92 us -> 12.3 us
  transfers between devices with their start and end apart: 6 -> 0, of which waited for: 6 -> 0; matrix products, arithmetic and copies ran while one was open for 9% -> 0% of each run, Pallas kernels for 0% -> 0%
where the time goes in v2:
time: 123 us
  Pallas kernels  110 us (89%)
  local copies, waits for them, and re-layouts  12.3 us (10%)
    pallas_call x1, Pallas kernels, local(): pl.pallas_call(main_kernel, out_shape=(jax.ShapeDtypeStruct((SEQ, D), BF)...  102 us
    unnamed x20, local copies, waits for them, and re-layouts  12.3 us
    pallas_call x1, Pallas kernels, local(): pl.pallas_call(close_kernel, grid=(steps,), out_shape=(jax.ShapeDtypeStru...  7.67 us

profile of v2, /device:TPU:1, one launch (start us, length us, event | category | flops | bytes accessed | tf_op | source)
XLA Modules:
  0.0 122.6 jit_solution(125966981173322400)
XLA Ops:
  0.6 0.0 copy-start.1
  0.6 1.1 copy-done.1
  1.8 0.0 copy-start.3
  1.8 1.1 copy-done.3
  2.9 0.0 copy-start.4
  2.9 1.1 copy-done.4
  4.0 0.0 copy-start.5
  4.0 1.0 copy-done.5
  5.0 0.0 copy-start.6
  5.0 1.0 copy-done.6
  6.0 0.0 copy-start.7
  6.0 0.9 copy-done.7
  6.9 0.0 copy-start.8
  6.9 0.9 copy-done.8
  7.8 0.0 copy-start.9
  7.8 0.9 copy-done.9
  8.7 102.0 %exchange.1 = (bf16[256,12288]{1,0:T(8,128)(2,1)}, bf16[4,256,768]{2,1,0:T(8,128)(2,1)}, bf16[256,384]{1,0:T(8,128)(2,1)S(1)}, bf16[256,384]{1,0:T(8,128)(2,1)S(...) custom-call(bf16[256,384]{1,0:T(8,128)(2,1)S(1)} %copy-done.7, bf16[256,384]{1,0:T(8,128)(2,1)S(1)} %copy-done.8, ...), custom_call_target="tpu_custom_call" | custom-call | tf_op jit(solution)/shard_map/exchange/pallas_call | solution.py:390
  110.7 0.0 copy-start
  110.7 2.8 %copy-done = bf16[256,12288]{1,0:T(8,128)(2,1)S(1)} copy-done((bf16[256,12288]{1,0:T(8,128)(2,1)S(1)}, bf16[256,12288]{1,0:T(8,128)(2,1)}, u32[]{:S(2)}) %copy-start) | copy-done | bytes 6291480
  113.5 0.0 copy-start.2
  113.5 1.4 %copy-done.2 = bf16[4,256,768]{2,1,0:T(8,128)(2,1)S(1)} copy-done((bf16[4,256,768]{2,1,0:T(8,128)(2,1)S(1)}, bf16[4,256,768]{2,1,0:T(8,128)(2,1)}, u32[]{:S(2)}) %copy-start.2) | copy-done | bytes 1572888
  114.9 7.7 %close.1 = (bf16[256,12288]{1,0:T(8,128)(2,1)}, bf16[256,384]{1,0:T(8,128)(2,1)}, bf16[256,384]{1,0:T(8,128)(2,1)}, bf16[256,384]{1,0:T(8,128)(2,1)}, f32[768,384]{1,0:T(8,128)}) custom-call(bf16[256,12288]{1,0:T(8,128)(2,1)S(1)} %copy-done, bf16[4,256,768]{2,1,0:T(8,128)(2,1)S(1)} %copy-done.2, bf16[3072,128]{1,0:T(8,128)(2,1)S(1)} %bitcast.2, ...), custom_call_target="tpu_custom_call" | custom-call | tf_op jit(solution)/shard_map/close/pallas_call | solution.py:433
Async XLA Ops:
  0.6 1.1 copy-start.1
  1.8 1.1 copy-start.3
  2.9 1.1 copy-start.4
  4.0 1.0 copy-start.5
  5.0 1.0 copy-start.6
  6.0 0.9 copy-start.7
  6.9 0.9 copy-start.8
  7.8 0.9 copy-start.9
  110.7 2.8 %copy-start = (bf16[256,12288]{1,0:T(8,128)(2,1)S(1)}, bf16[256,12288]{1,0:T(8,128)(2,1)}, u32[]{:S(2)}) copy-start(bf16[256,12288]{1,0:T(8,128)(2,1)} %get-tuple-element.11.resid_ref) | copy-start | bytes 18874372
  113.5 1.4 %copy-start.2 = (bf16[4,256,768]{2,1,0:T(8,128)(2,1)S(1)}, bf16[4,256,768]{2,1,0:T(8,128)(2,1)}, u32[]{:S(2)}) copy-start(bf16[4,256,768]{2,1,0:T(8,128)(2,1)} %get-tuple-element.12.cs_ref) | copy-start | bytes 4718596

commit v3 on v2

v3 whole, which is shorter than its diff:
```python
import math

import jax
import jax.numpy as jnp
from jax import lax
from jax.experimental import pallas as pl
from jax.experimental.pallas import tpu as pltpu
from jax.sharding import PartitionSpec as P

HD = 128
NEG_FILL = -1e30
MESH = pl.DeviceIdType.MESH
BF, F32 = jnp.bfloat16, jnp.float32

NX, NZL, NY, NZH, NC = 4, 4, 4, 2, 2
TB = 16
SEQ = 256
HEADS = 3
AW = HEADS * HD
NBLK, CODE_W, BLOCK = 96, 32, 128
CODE = NBLK * CODE_W
D = NBLK * BLOCK
OWN = 6
ER = OWN * CODE_W
CH = NX * ER
HALF = SEQ // NC
PAIR = TB * NZH


def nt(a, b):
    return lax.dot_general(a, b, (((1,), (1,)), ((), ())), preferred_element_type=F32)


def nn(a, b):
    return lax.dot_general(a, b, (((1,), (0,)), ((), ())), preferred_element_type=F32)


def tn(a, b):
    return lax.dot_general(a, b, (((0,), (0,)), ((), ())), preferred_element_type=F32)


def place(t):
    return ((t % NC) * NY + t // (NC * NZH)) * NZH + (t // NC) % NZH


class Sems:
    def __init__(self, send, recv):
        self.send, self.recv, self.used, self.started = send, recv, 0, []

    def copy(self, src, dst, target):
        i = self.used
        self.used += 1
        made = pltpu.make_async_remote_copy(
            src_ref=src,
            dst_ref=dst,
            send_sem=self.send.at[i],
            recv_sem=self.recv.at[i],
            device_id=target,
            device_id_type=MESH,
        )
        made.start()
        self.started.append(made)
        return made


N_SEMS = 160
G_ORDER = (2, 1, 3, 0)
STEPS = (1, 3, 2)
PIECES = 2


def wait_for(ref, send_sem, recv_sem, target):
    pltpu.make_async_remote_copy(
        src_ref=ref,
        dst_ref=ref,
        send_sem=send_sem,
        recv_sem=recv_sem,
        device_id=target,
        device_id_type=MESH,
    ).wait_recv()


def main_kernel(
    q_hbm, k_hbm, v_hbm, res_ref, w_hbm, enc_hbm, dec_hbm, go_hbm,
    resid_ref, ag, dq_ref, dk_ref, dv_ref, gw_ref,
    q_ref, k_ref, v_ref, w_ref, enc, dec_ref, go_ref,
    ew, gcb, attn_p, probs, ga,
    c_own, c_send, c_recv, y_sum, y_recv, z_sum, z_recv,
    gp, g_via, g_mid, g_near, g_far, g_sum, gz_recv,
    send_sem, recv_sem, line_send, line_recv, local_sem,
):
    dp, t = lax.axis_index("dp"), lax.axis_index("tensor")
    zl, x = dp // NX, dp % NX
    y, zh, c = t // (NZH * NC), (t // NC) % NZH, t % NC

    def to_x(k):
        return (zl * NX + (x + k) % NX, t)

    def to_zl(k):
        return (((zl + k) % NZL) * NX + x, t)

    def to_y(k):
        return (dp, (((y + k) % NY) * NZH + zh) * NC + c)

    to_zh = (dp, (y * NZH + 1 - zh) * NC + c)
    to_c = (dp, (y * NZH + zh) * NC + 1 - c)

    sems = Sems(send_sem, recv_sem)
    send = sems.copy

    barrier = pltpu.get_barrier_semaphore()
    peers = [to_x(1), to_x(3)] + [to_zl(k) for k in STEPS]
    peers += [to_y(k) for k in STEPS] + [to_zh, to_c]
    for peer in peers:
        pl.semaphore_signal(barrier, inc=1, device_id=peer, device_id_type=MESH)

    own_rows = pl.ds(pl.multiple_of(t * TB, TB), TB)
    loads = {}
    for i, (name, src, dst) in enumerate((
        ("enc", enc_hbm.at[pl.ds(dp * OWN, OWN)], enc),
        ("w", w_hbm, w_ref),
        ("go", go_hbm, go_ref),
        ("dec", dec_hbm, dec_ref),
        ("q", q_hbm, q_ref),
        ("k", k_hbm, k_ref),
        ("v", v_hbm, v_ref),
        ("res", res_ref, resid_ref.at[own_rows]),
    )):
        loads[name] = pltpu.make_async_copy(src, dst, local_sem.at[i])
        loads[name].start()

    def ew_at(zl_, x_):
        return ew.at[zl_, pl.ds(pl.multiple_of(x_ * ER, ER), ER)]

    loads["enc"].wait()
    loads["w"].wait()
    for b in range(OWN):
        rows = pl.ds(pl.multiple_of(x * ER + b * CODE_W, CODE_W), CODE_W)
        ew[zl, rows, :] = nn(enc[b], w_ref[b * BLOCK : (b + 1) * BLOCK, :]).astype(BF)
    pl.semaphore_wait(barrier, len(peers))

    zls = [zl, zl + 1 - 2 * (zl % 2), 2 - zl // 2, 3 - 3 * (zl // 2)]

    def line_copy(slot, z_, step):
        return pltpu.make_async_remote_copy(
            src_ref=ew_at(z_, x),
            dst_ref=ew_at(z_, x),
            send_sem=line_send.at[slot],
            recv_sem=line_recv.at[z_],
            device_id=((zl + step) * NX + x, t),
            device_id_type=MESH,
        )

    line = [(zl < NZL - 1, 0, zl, 1), (zl > 0, 1, zl, -1)]
    for i in range(1, NZL):
        up = zls[i] < zl
        goes = jnp.logical_or(
            jnp.logical_and(up, zl < NZL - 1), jnp.logical_and(jnp.logical_not(up), zl > 0)
        )
        line.append((goes, 1 + i, zls[i], jnp.where(up, 1, -1)))

    def line_start(goes, *rest):
        @pl.when(goes)
        def _():
            line_copy(*rest).start()

    for entry in line[:2]:
        line_start(*entry)
    e_up, e_down, e_far = {}, {}, {}

    def weight_x(i):
        e_up[i] = send(ew_at(zls[i], x), ew_at(zls[i], x), to_x(1))
        e_down[i] = send(ew_at(zls[i], x), ew_at(zls[i], x), to_x(3))

    def weight_x2(i):
        if i % 2 == 0:
            e_up[i].wait_recv()
            at = ew_at(zls[i], (x + 3) % NX)
            e_far[i] = send(at, at, to_x(1))
        else:
            e_down[i].wait_recv()
            at = ew_at(zls[i], (x + 1) % NX)
            e_far[i] = send(at, at, to_x(3))

    weight_x(0)

    def place_of(y_, zh_, c_):
        return (c_ * NY + y_) * NZH + zh_

    def block_rows(p, n=1):
        return pl.ds(pl.multiple_of(p * TB, TB), TB * n)

    mine = block_rows(place_of(y, zh, c))
    other = block_rows(place_of(y, 1 - zh, c))
    lane_block = lax.broadcasted_iota(jnp.int32, (TB, BLOCK), 1) // CODE_W
    loads["res"].wait()
    loads["go"].wait()
    loads["dec"].wait()
    for g in range(NBLK // 4):
        wide = jnp.concatenate(
            [go_ref[:, (4 * g + j) * BLOCK : (4 * g + j + 1) * BLOCK] for j in range(4)], axis=0
        )
        coded = nt(wide, dec_ref[g * BLOCK : (g + 1) * BLOCK, :])
        picked = coded[:TB]
        for j in range(1, 4):
            picked = jnp.where(lane_block == j, coded[j * TB : (j + 1) * TB], picked)
        gcb[g // 6, mine, (g % 6) * BLOCK : (g % 6 + 1) * BLOCK] = picked.astype(BF)

    gc_y, gc_c = {}, []
    gc_z = send(gcb.at[:, mine], gcb.at[:, mine], to_zh)
    for k in STEPS:
        gc_y[k, 0] = send(gcb.at[:, mine], gcb.at[:, mine], to_y(k))

    def cotangent_y():
        gc_z.wait_recv()
        for k in STEPS:
            gc_y[k, 1] = send(gcb.at[:, other], gcb.at[:, other], to_y(k))
        pair = block_rows(place_of(y, 0, c), NZH)
        gc_c.append(send(gcb.at[:, pair], gcb.at[:, pair], to_c))

    def cotangent_c():
        for k in STEPS:
            gc_y[k, 0].wait_recv()
            gc_y[k, 1].wait_recv()
            pair = block_rows(place_of((y - k + NY) % NY, 0, c), NZH)
            gc_c.append(send(gcb.at[:, pair], gcb.at[:, pair], to_c))
        for made in gc_c:
            made.wait_recv()

    def res_at(y_, zh_, p):
        rows = pl.ds(pl.multiple_of((y_ * NZH + zh_) * (NC * TB) + c * TB, TB), TB)
        return resid_ref.at[rows, p * (D // PIECES) : (p + 1) * (D // PIECES)]

    res, res_c = {}, []
    shards = (zh, 1 - zh)

    def res_move(name, y_, i, p, target):
        at = res_at(y_, shards[i], p)
        res[name, i, p] = send(at, at, target)

    def res_core(y_, i, p):
        at = res_at(y_, shards[i], p)
        res_c.append(send(at, at, to_c))

    def res_z(p):
        res_move("z", y, 0, p, to_zh)

    def res_first(i, p):
        if i:
            res["z", 0, p].wait_recv()
        res_move("up", y, i, p, to_y(1))
        res_move("down", y, i, p, to_y(3))

    def res_second(i, p):
        res["up", i, p].wait_recv()
        if p % 2 == 0:
            res_move("far", (y + 3) % NY, i, p, to_y(1))
        res["down", i, p].wait_recv()
        if p % 2:
            res_move("far", (y + 1) % NY, i, p, to_y(3))

    def res_cores(i, p):
        res_core(y, i, p)
        res_core((y + 3) % NY, i, p)
        res_core((y + 1) % NY, i, p)

    def res_last(i, p):
        res["far", i, p].wait_recv()
        res_core((y + 2) % NY, i, p)

    scale = 1.0 / math.sqrt(HD)

    def attention_forward():
        for name in "qkv":
            loads[name].wait()
        row_index = lax.broadcasted_iota(jnp.int32, (SEQ, SEQ), 0)
        col_index = lax.broadcasted_iota(jnp.int32, (SEQ, SEQ), 1)
        for h in range(HEADS):
            cols = slice(h * HD, (h + 1) * HD)
            scores = nt(q_ref[:, cols], k_ref[:, cols]) * scale
            scores = jnp.where(col_index <= row_index, scores, NEG_FILL)
            weights = jnp.exp(scores - jnp.max(scores, axis=-1, keepdims=True))
            prob = weights / jnp.sum(weights, axis=-1, keepdims=True)
            probs[h] = prob
            mixed = nn(prob.astype(BF), v_ref[:, cols]).astype(BF)
            for b in range(SEQ // TB):
                p = place(b)
                attn_p[p * TB : (p + 1) * TB, cols] = mixed[b * TB : (b + 1) * TB]

    def attention_backward():
        for h in range(HEADS):
            cols = slice(h * HD, (h + 1) * HD)
            grad = jnp.concatenate(
                [ga[place(b) * TB : (place(b) + 1) * TB, cols] for b in range(SEQ // TB)], axis=0
            ).astype(BF)
            prob = probs[h]
            dprobs = nt(grad, v_ref[:, cols])
            center = jnp.sum(dprobs * prob, axis=-1, keepdims=True)
            grad_scores = (prob * (dprobs - center) * scale).astype(BF)
            dq_ref[:, cols] = nn(grad_scores, k_ref[:, cols]).astype(BF)
            dk_ref[:, cols] = tn(grad_scores, q_ref[:, cols]).astype(BF)
            dv_ref[:, cols] = tn(prob.astype(BF), grad).astype(BF)

    g_up, g_down, g_on, gz = {}, {}, {}, {}

    def grad_start(i):
        z_ = (zl + G_ORDER[i]) % NZL
        term = tn(gcb[z_], attn_p[...])
        for x_ in range(NX):
            gp[i, x_] = term[x_ * ER : (x_ + 1) * ER].astype(BF)
        far = gp.at[i, (x + 2) % NX]
        if i % 2 == 0:
            g_up[i] = send(far, g_via.at[i], to_x(1))
            g_down[i] = send(gp.at[i, (x + 3) % NX], g_near.at[i], to_x(3))
        else:
            g_down[i] = send(far, g_via.at[i], to_x(3))
            g_up[i] = send(gp.at[i, (x + 1) % NX], g_near.at[i], to_x(1))

    def grad_on(i):
        step = 1 if i % 2 == 0 else 3
        (g_up if i % 2 == 0 else g_down)[i].wait_recv()
        g_mid[i] = (gp[i, (x + step) % NX].astype(F32) + g_via[i].astype(F32)).astype(BF)
        g_on[i] = send(g_mid.at[i], g_far.at[i], to_x(step))

    def grad_z(i):
        (g_down if i % 2 == 0 else g_up)[i].wait_recv()
        g_on[i].wait_recv()
        total = gp[i, x].astype(F32) + g_near[i].astype(F32) + g_far[i].astype(F32)
        g_sum[i] = total.astype(BF)
        k = G_ORDER[i]
        if k:
            gz[k] = send(g_sum.at[i], gz_recv.at[k - 1], to_zl(k))

    def grad_end():
        total = g_sum[G_ORDER.index(0)].astype(F32)
        for k in STEPS:
            gz[k].wait_recv()
            total += gz_recv[k - 1].astype(F32)
        summed = total.astype(BF)
        for b in range(OWN):
            gw_ref[b * BLOCK : (b + 1) * BLOCK, :] = tn(
                enc[b], summed[b * CODE_W : (b + 1) * CODE_W]
            )

    c_cp, y_cp, z_cp, a_cp, ac_cp = {}, {}, {}, {}, {}

    def code(i):
        (e_down if i % 2 == 0 else e_up)[i].wait_recv()
        e_far[i].wait_recv()
        codes = nt(attn_p[...], ew[zls[i]]).astype(BF)
        for half in range(NC):
            part = codes[half * HALF : (half + 1) * HALF]

            @pl.when(c == half)
            def _():
                c_own[i] = part

            @pl.when(c != half)
            def _():
                c_send[i] = part

        c_cp[i] = send(c_send.at[i], c_recv.at[i], to_c)

    def grad_attn(i):
        grown = nn(gcb[zls[i]], ew[zls[i]])
        if i == 0:
            ga[...] = grown
        else:
            ga[...] += grown

    def code_y(i):
        c_cp[i].wait_recv()
        y_sum[i] = (c_own[i].astype(F32) + c_recv[i].astype(F32)).astype(BF)
        for k in STEPS:
            rows = pl.ds(pl.multiple_of(((y + k) % NY) * PAIR, PAIR), PAIR)
            y_cp[i, k] = send(y_sum.at[i, rows], y_recv.at[i, k - 1], to_y(k))

    def code_z(i):
        for k in STEPS:
            y_cp[i, k].wait_recv()
        rows = pl.ds(pl.multiple_of(y * PAIR, PAIR), PAIR)
        total = y_sum[i, rows].astype(F32)
        for k in range(3):
            total += y_recv[i, k].astype(F32)
        z_sum[i] = total.astype(BF)
        z_cp[i] = send(z_sum.at[i], z_recv.at[i], to_zh)

    def ag_at(z_, y_):
        return ag.at[z_, pl.ds(pl.multiple_of((c * NY + y_) * PAIR, PAIR), PAIR)]

    def code_back(i):
        z_cp[i].wait_recv()
        at = ag_at(zls[i], y)
        at[...] = (z_sum[i].astype(F32) + z_recv[i].astype(F32)).astype(BF)
        for k in STEPS:
            a_cp[i, k] = send(at, at, to_y(k))
        ac_cp[i, 0] = send(at, at, to_c)

    def code_out(i):
        for k in STEPS:
            a_cp[i, k].wait_recv()
            at = ag_at(zls[i], (y - k + NY) % NY)
            ac_cp[i, k] = send(at, at, to_c)

    def code_done(i):
        for k in (0,) + STEPS:
            ac_cp[i, k].wait_recv()

    def weight_z(i):
        at = ew_at(zls[i], x)
        wait_for(at, line_send.at[0], line_recv.at[zls[i]], to_zl(1))
        line_start(*line[1 + i])
        weight_x(i)

    res_first(0, 0)
    attention_forward()
    weight_x2(0)
    weight_z(1)
    weight_z(2)
    code(0)
    weight_x2(1)
    cotangent_y()
    weight_z(3)
    res_z(0)
    res_first(0, 1)
    code_y(0)
    res_second(0, 0)
    res_cores(0, 0)
    weight_x2(2)
    code(1)
    cotangent_c()
    res_z(1)
    grad_start(0)
    code_y(1)
    code_z(0)
    weight_x2(3)
    code(2)
    code_y(2)
    grad_attn(0)
    grad_attn(1)
    grad_attn(2)
    code(3)
    grad_start(1)
    code_y(3)
    grad_on(0)
    grad_start(2)
    grad_start(3)
    code_z(1)
    res_second(0, 1)
    res_cores(0, 1)
    code_z(2)
    res_first(1, 0)
    code_back(0)
    grad_on(1)
    grad_attn(3)
    attention_backward()
    code_z(3)
    grad_z(0)
    grad_on(2)
    code_back(1)
    code_out(0)
    res_first(1, 1)
    grad_z(1)
    grad_on(3)
    code_back(2)
    res_second(1, 0)
    res_cores(1, 0)
    code_out(1)
    grad_z(2)
    grad_z(3)
    code_back(3)
    res_last(0, 0)
    res_last(0, 1)
    code_out(2)
    res_second(1, 1)
    res_cores(1, 1)
    code_out(3)
    for i in range(NZL):
        code_done(i)
    grad_end()
    res_last(1, 0)
    res_last(1, 1)

    for made in res_c:
        made.wait_recv()
    for goes, *rest in line:

        @pl.when(goes)
        def _():
            line_copy(*rest).wait_send()

    for made in sems.started:
        made.wait_send()


STEP_BLOCKS = 8
CLOSE_STEPS = NBLK // STEP_BLOCKS


def close_kernel(
    resid_ref, cs_ref, dec_hbm, dq_in, dk_in, dv_in, gw_in,
    out_ref, dq_ref, dk_ref, dv_ref, gw_ref, dec_ref, layer, copy_sem, out_sem,
):
    load = pltpu.make_async_copy(dec_hbm, dec_ref, copy_sem.at[4])
    load.start()
    copies = [
        pltpu.make_async_copy(src, dst, copy_sem.at[i])
        for i, (src, dst) in enumerate(
            ((dq_in, dq_ref), (dk_in, dk_ref), (dv_in, dv_ref), (gw_in, gw_ref))
        )
    ]
    for copy in copies:
        copy.start()
    load.wait()
    depth, width = STEP_BLOCKS * CODE_W, STEP_BLOCKS * BLOCK
    per = CLOSE_STEPS // NZL
    row = lax.broadcasted_iota(jnp.int32, (depth, BLOCK), 0) // CODE_W
    for step in range(CLOSE_STEPS):
        cols = slice(step * width, (step + 1) * width)
        dec = dec_ref[step * depth : (step + 1) * depth, :]
        opened = jnp.concatenate(
            [jnp.where(row == b, dec, jnp.zeros_like(dec)) for b in range(STEP_BLOCKS)], axis=1
        )
        codes = cs_ref[step // per, :, (step % per) * depth : (step % per + 1) * depth]
        added = nn(codes, opened)
        for b in range(SEQ // TB):
            p = place(b)
            rows = slice(b * TB, (b + 1) * TB)
            layer[rows, cols] = (
                resid_ref[rows, cols].astype(F32) + added[p * TB : (p + 1) * TB]
            ).astype(BF)
        copies.append(
            pltpu.make_async_copy(layer.at[:, cols], out_ref.at[:, cols], out_sem.at[step])
        )
        copies[-1].start()
    for copy in copies:
        copy.wait()


def local(queries, key_rows, value_rows, residual_in, out_weight, encoder, decoder, grad_out):
    vmem = pl.BlockSpec(memory_space=pltpu.VMEM)
    anywhere = pl.BlockSpec(memory_space=pl.ANY)
    dec_rows = decoder.reshape(CODE, BLOCK)
    operands = (queries, key_rows, value_rows, residual_in, out_weight, encoder, dec_rows, grad_out)
    operands = [pltpu.with_memory_space_constraint(a, pltpu.HBM) for a in operands]
    dec_rows = operands[6]
    resid, code_sum, dq, dk, dv, gw = pl.pallas_call(
        main_kernel,
        out_shape=(
            pltpu.VMEM((SEQ, D), BF),
            pltpu.VMEM((NZL, SEQ, CH), BF),
            pltpu.VMEM((SEQ, AW), BF),
            pltpu.VMEM((SEQ, AW), BF),
            pltpu.VMEM((SEQ, AW), BF),
            pltpu.VMEM((OWN * BLOCK, AW), F32),
        ),
        in_specs=[anywhere] * 8,
        out_specs=(vmem,) * 6,
        scratch_shapes=[
            pltpu.VMEM((SEQ, AW), BF),
            pltpu.VMEM((SEQ, AW), BF),
            pltpu.VMEM((SEQ, AW), BF),
            pltpu.VMEM((OWN * BLOCK, AW), BF),
            pltpu.VMEM((OWN, CODE_W, BLOCK), BF),
            pltpu.VMEM((CODE, BLOCK), BF),
            pltpu.VMEM((TB, D), BF),
            pltpu.VMEM((NZL, CH, AW), BF),
            pltpu.VMEM((NZL, SEQ, CH), BF),
            pltpu.VMEM((SEQ, AW), BF),
            pltpu.VMEM((HEADS, SEQ, SEQ), F32),
            pltpu.VMEM((SEQ, AW), F32),
            pltpu.VMEM((4, HALF, CH), BF),
            pltpu.VMEM((4, HALF, CH), BF),
            pltpu.VMEM((4, HALF, CH), BF),
            pltpu.VMEM((4, HALF, CH), BF),
            pltpu.VMEM((4, 3, PAIR, CH), BF),
            pltpu.VMEM((4, PAIR, CH), BF),
            pltpu.VMEM((4, PAIR, CH), BF),
            pltpu.VMEM((NZL, NX, ER, AW), BF),
            pltpu.VMEM((NZL, ER, AW), BF),
            pltpu.VMEM((NZL, ER, AW), BF),
            pltpu.VMEM((NZL, ER, AW), BF),
            pltpu.VMEM((NZL, ER, AW), BF),
            pltpu.VMEM((NZL, ER, AW), BF),
            pltpu.VMEM((3, ER, AW), BF),
            pltpu.SemaphoreType.DMA((N_SEMS,)),
            pltpu.SemaphoreType.DMA((N_SEMS,)),
            pltpu.SemaphoreType.DMA((5,)),
            pltpu.SemaphoreType.DMA((NZL,)),
            pltpu.SemaphoreType.DMA((8,)),
        ],
        name="exchange",
        compiler_params=pltpu.CompilerParams(
            collective_id=0, has_side_effects=True, vmem_limit_bytes=32 * 2**20
        ),
    )(*operands)

    return pl.pallas_call(
        close_kernel,
        out_shape=(
            pltpu.HBM((SEQ, D), BF),
            pltpu.HBM((SEQ, AW), BF),
            pltpu.HBM((SEQ, AW), BF),
            pltpu.HBM((SEQ, AW), BF),
            pltpu.HBM((OWN * BLOCK, AW), F32),
        ),
        in_specs=[vmem, vmem, anywhere, vmem, vmem, vmem, vmem],
        out_specs=(anywhere,) * 5,
        scratch_shapes=[
            pltpu.VMEM((CODE, BLOCK), BF),
            pltpu.VMEM((SEQ, D), BF),
            pltpu.SemaphoreType.DMA((5,)),
            pltpu.SemaphoreType.DMA((CLOSE_STEPS,)),
        ],
        name="close",
        compiler_params=pltpu.CompilerParams(vmem_limit_bytes=20 * 2**20),
    )(resid, code_sum, dec_rows, dq, dk, dv, gw)


def solution(mesh):
    placed = (
        P("dp", "tensor"),
        P("dp", "tensor"),
        P("dp", "tensor"),
        P(("dp", "tensor"), None),
        P("dp", "tensor"),
        P(),
        P(),
        P(("dp", "tensor"), None),
    )
    return jax.shard_map(
        local,
        mesh=mesh,
        in_specs=placed,
        out_specs=(
            P("dp", None),
            P("dp", "tensor"),
            P("dp", "tensor"),
            P("dp", "tensor"),
            P("dp", "tensor"),
        ),
        check_vma=False,
    )
```

time: 123 us -> 85.2 us (0.69)
  Pallas kernels: 110 us -> 84.4 us
  local copies, waits for them, and re-layouts: 12.3 us -> 0 us
    pallas_call x2, Pallas kernels: 110 us -> 84.4 us  [the longest x1 79.6 us: local(): pl.pallas_call(main_kernel, out_shape=(pltpu.VMEM((SEQ, D), BF), pltpu.VM...]
    unnamed x20 -> x0, local copies, waits for them, and re-layouts: 12.3 us -> none
where the time goes in v3:
time: 85.2 us; the launch traced here: 85.1 us
  Pallas kernels  84.4 us (99%)
    pallas_call x1, Pallas kernels, local(): pl.pallas_call(main_kernel, out_shape=(pltpu.VMEM((SEQ, D), BF), pltpu.VM...  79.6 us
    pallas_call x1, Pallas kernels, local(): pl.pallas_call(close_kernel, out_shape=(pltpu.HBM((SEQ, D), BF), pltpu.HB...  4.79 us

profile of v3, /device:TPU:1, one launch (start us, length us, event | category | flops | bytes accessed | tf_op | source)
XLA Modules:
  0.0 85.1 jit_solution(8002995971117883701)
XLA Ops:
  0.6 79.6 %exchange.1 = (bf16[256,12288]{1,0:T(8,128)(2,1)S(1)}, bf16[4,256,768]{2,1,0:T(8,128)(2,1)S(1)}, bf16[256,384]{1,0:T(8,128)(2,1)S(1)}, bf16[256,384]{1,0:T(8,128...) custom-call(bf16[256,384]{1,0:T(8,128)(2,1)} %q_hbm.1, bf16[256,384]{1,0:T(8,128)(2,1)} %k_hbm.1, ...), custom_call_target="tpu_custom_call" | custom-call | tf_op jit(solution)/shard_map/exchange/pallas_call | solution.py:547
  80.3 4.8 %close.1 = (bf16[256,12288]{1,0:T(8,128)(2,1)}, bf16[256,384]{1,0:T(8,128)(2,1)}, bf16[256,384]{1,0:T(8,128)(2,1)}, bf16[256,384]{1,0:T(8,128)(2,1)}, f32[768,384]{1,0:T(8,128)}) custom-call(bf16[256,12288]{1,0:T(8,128)(2,1)S(1)} %get-tuple-element.11.resid_ref, bf16[4,256,768]{2,1,0:T(8,128)(2,1)S(1)} %get-tuple-element.12.cs_ref, ...), custom_call_target="tpu_custom_call" | custom-call | tf_op jit(solution)/shard_map/close/pallas_call | solution.py:598

commit v4 on v3

--- a/solution.py
+++ b/solution.py
@@ -43,18 +43,28 @@
     return ((t % NC) * NY + t // (NC * NZH)) * NZH + (t // NC) % NZH
 
 
+N_SEND, N_RECV = 48, 96
+
+
 class Sems:
     def __init__(self, send, recv):
-        self.send, self.recv, self.used, self.started = send, recv, 0, []
-
-    def copy(self, src, dst, target):
-        i = self.used
-        self.used += 1
+        self.send, self.recv, self.groups, self.used, self.started = send, recv, {}, 0, []
+
+    def slot(self, group):
+        if group not in self.groups:
+            self.groups[group] = self.used
+            self.used += 1
+        return self.recv.at[self.groups[group]]
+
+    def copy(self, src, dst, target, group=None):
+        n = len(self.started)
+        if n >= N_SEND:
+            self.started[n - N_SEND].wait_send()
         made = pltpu.make_async_remote_copy(
             src_ref=src,
             dst_ref=dst,
-            send_sem=self.send.at[i],
-            recv_sem=self.recv.at[i],
+            send_sem=self.send.at[n % N_SEND],
+            recv_sem=self.slot(n if group is None else group),
             device_id=target,
             device_id_type=MESH,
         )
@@ -62,11 +72,12 @@
         self.started.append(made)
         return made
 
-
-N_SEMS = 160
-G_ORDER = (2, 1, 3, 0)
+    def arrived(self, ref, group, target):
+        wait_for(ref, self.send.at[0], self.slot(group), target)
+
+G_ORDER = (1, 3, 2, 0)
 STEPS = (1, 3, 2)
-PIECES = 2
+PIECES = 4
 
 
 def wait_for(ref, send_sem, recv_sem, target):
@@ -82,12 +93,12 @@
 
 def main_kernel(
     q_hbm, k_hbm, v_hbm, res_ref, w_hbm, enc_hbm, dec_hbm, go_hbm,
-    resid_ref, ag, dq_ref, dk_ref, dv_ref, gw_ref,
-    q_ref, k_ref, v_ref, w_ref, enc, dec_ref, go_ref,
+    resid_ref, ag, dq_ref, dk_ref, dv_ref, gw_ref, dec_ref,
+    q_ref, k_ref, v_ref, w_ref, enc, go_ref,
     ew, gcb, attn_p, probs, ga,
-    c_own, c_send, c_recv, y_sum, y_recv, z_sum, z_recv,
-    gp, g_via, g_mid, g_near, g_far, g_sum, gz_recv,
-    send_sem, recv_sem, line_send, line_recv, local_sem,
+    c_own, c_send, c_recv, y_sum, y_via, y_mid, y_near, y_far, z_sum, z_recv,
+    gp, g_via, g_mid, g_near, g_far, g_sum, gz_recv, gz_via,
+    send_sem, recv_sem, line_send, line_recv, gz_send, gz_arrive, local_sem,
 ):
     dp, t = lax.axis_index("dp"), lax.axis_index("tensor")
     zl, x = dp // NX, dp % NX
@@ -110,7 +121,7 @@
 
     barrier = pltpu.get_barrier_semaphore()
     peers = [to_x(1), to_x(3)] + [to_zl(k) for k in STEPS]
-    peers += [to_y(k) for k in STEPS] + [to_zh, to_c]
+    peers += [to_y(1), to_y(3), to_zh, to_c]
     for peer in peers:
         pl.semaphore_signal(barrier, inc=1, device_id=peer, device_id_type=MESH)
 
@@ -206,41 +217,58 @@
             picked = jnp.where(lane_block == j, coded[j * TB : (j + 1) * TB], picked)
         gcb[g // 6, mine, (g % 6) * BLOCK : (g % 6 + 1) * BLOCK] = picked.astype(BF)
 
-    gc_y, gc_c = {}, []
+    gc_up, gc_down, gc_far = {}, {}, {}
     gc_z = send(gcb.at[:, mine], gcb.at[:, mine], to_zh)
-    for k in STEPS:
-        gc_y[k, 0] = send(gcb.at[:, mine], gcb.at[:, mine], to_y(k))
+
+    def cotangent_first(i):
+        at = gcb.at[:, (mine, other)[i]]
+        gc_up[i] = send(at, at, to_y(1))
+        gc_down[i] = send(at, at, to_y(3))
+
+    def cotangent_core(y_):
+        at = gcb.at[:, block_rows(place_of(y_, 0, c), NZH)]
+        send(at, at, to_c, "gc")
 
     def cotangent_y():
         gc_z.wait_recv()
-        for k in STEPS:
-            gc_y[k, 1] = send(gcb.at[:, other], gcb.at[:, other], to_y(k))
-        pair = block_rows(place_of(y, 0, c), NZH)
-        gc_c.append(send(gcb.at[:, pair], gcb.at[:, pair], to_c))
+        cotangent_first(1)
+        cotangent_core(y)
+
+    def cotangent_relay():
+        gc_up[0].wait_recv()
+        at = gcb.at[:, block_rows(place_of((y + 3) % NY, zh, c))]
+        gc_far[0] = send(at, at, to_y(1))
+        gc_down[0].wait_recv()
+        gc_down[1].wait_recv()
+        at = gcb.at[:, block_rows(place_of((y + 1) % NY, 1 - zh, c))]
+        gc_far[1] = send(at, at, to_y(3))
+        cotangent_core((y + 1) % NY)
+        gc_up[1].wait_recv()
+        cotangent_core((y + 3) % NY)
 
     def cotangent_c():
-        for k in STEPS:
-            gc_y[k, 0].wait_recv()
-            gc_y[k, 1].wait_recv()
-            pair = block_rows(place_of((y - k + NY) % NY, 0, c), NZH)
-            gc_c.append(send(gcb.at[:, pair], gcb.at[:, pair], to_c))
-        for made in gc_c:
-            made.wait_recv()
+        gc_far[0].wait_recv()
+        gc_far[1].wait_recv()
+        cotangent_core((y + 2) % NY)
+        sems.arrived(gcb.at[:, :HALF], "gc", to_c)
+
+    cotangent_first(0)
 
     def res_at(y_, zh_, p):
         rows = pl.ds(pl.multiple_of((y_ * NZH + zh_) * (NC * TB) + c * TB, TB), TB)
         return resid_ref.at[rows, p * (D // PIECES) : (p + 1) * (D // PIECES)]
 
-    res, res_c = {}, []
+    res = {}
     shards = (zh, 1 - zh)
 
     def res_move(name, y_, i, p, target):
         at = res_at(y_, shards[i], p)
         res[name, i, p] = send(at, at, target)
 
-    def res_core(y_, i, p):
-        at = res_at(y_, shards[i], p)
-        res_c.append(send(at, at, to_c))
+    def res_core(y_, i, half):
+        rows = pl.ds(pl.multiple_of((y_ * NZH + shards[i]) * (NC * TB) + c * TB, TB), TB)
+        at = resid_ref.at[rows, half * (D // 2) : (half + 1) * (D // 2)]
+        send(at, at, to_c, "res")
 
     def res_z(p):
         res_move("z", y, 0, p, to_zh)
@@ -259,18 +287,21 @@
         if p % 2:
             res_move("far", (y + 1) % NY, i, p, to_y(3))
 
-    def res_cores(i, p):
-        res_core(y, i, p)
-        res_core((y + 3) % NY, i, p)
-        res_core((y + 1) % NY, i, p)
-
-    def res_last(i, p):
-        res["far", i, p].wait_recv()
-        res_core((y + 2) % NY, i, p)
+    def res_cores(i, half):
+        res_core(y, i, half)
+        res_core((y + 3) % NY, i, half)
+        res_core((y + 1) % NY, i, half)
+
+    def res_last(i, half):
+        for p in (2 * half, 2 * half + 1):
+            res["far", i, p].wait_recv()
+        res_core((y + 2) % NY, i, half)
 
     scale = 1.0 / math.sqrt(HD)
 
     def attention_forward():
+        grad_slot(1, True)
+        grad_slot(3, True)
         for name in "qkv":
             loads[name].wait()
         row_index = lax.broadcasted_iota(jnp.int32, (SEQ, SEQ), 0)
@@ -301,7 +332,7 @@
             dk_ref[:, cols] = tn(grad_scores, q_ref[:, cols]).astype(BF)
             dv_ref[:, cols] = tn(prob.astype(BF), grad).astype(BF)
 
-    g_up, g_down, g_on, gz = {}, {}, {}, {}
+    g_up, g_down, g_on = {}, {}, {}
 
     def grad_start(i):
         z_ = (zl + G_ORDER[i]) % NZL
@@ -328,13 +359,50 @@
         total = gp[i, x].astype(F32) + g_near[i].astype(F32) + g_far[i].astype(F32)
         g_sum[i] = total.astype(BF)
         k = G_ORDER[i]
+        if k == 2:
+            @pl.when(inner)
+            def _():
+                wait_for(gz_via, gz_send.at[0], gz_arrive.at[3], to_zl(1))
+                g_sum[i] = (total + gz_via[...].astype(F32)).astype(BF)
+
         if k:
-            gz[k] = send(g_sum.at[i], gz_recv.at[k - 1], to_zl(k))
+            ends = zl == (-1, NZL - 1, -1, 0)[k]
+            step = {1: -1, 3: 1, 2: 0}[k]
+
+            @pl.when(jnp.logical_not(ends))
+            def _():
+                grad_copy(i, gz_recv.at[k - 1], k - 1, to_zl(k)).start()
+
+            @pl.when(ends)
+            def _():
+                grad_copy(i, gz_via, 3, ((zl + step) * NX + x, t)).start()
+
+    inner = jnp.logical_and(zl > 0, zl < NZL - 1)
+
+    def grad_copy(i, dst, slot, target):
+        return pltpu.make_async_remote_copy(
+            src_ref=g_sum.at[i],
+            dst_ref=dst,
+            send_sem=gz_send.at[i],
+            recv_sem=gz_arrive.at[slot],
+            device_id=target,
+            device_id_type=MESH,
+        )
+
+    def grad_slot(k, first):
+        lone = zl == {1: 0, 2: -1, 3: NZL - 1}[k]
+
+        @pl.when(lone if first else jnp.logical_not(lone))
+        def _():
+            if first:
+                gz_recv[k - 1] = jnp.zeros((ER, AW), BF)
+            else:
+                wait_for(gz_recv.at[k - 1], gz_send.at[0], gz_arrive.at[k - 1], to_zl(1))
 
     def grad_end():
         total = g_sum[G_ORDER.index(0)].astype(F32)
         for k in STEPS:
-            gz[k].wait_recv()
+            grad_slot(k, False)
             total += gz_recv[k - 1].astype(F32)
         summed = total.astype(BF)
         for b in range(OWN):
@@ -342,7 +410,7 @@
                 enc[b], summed[b * CODE_W : (b + 1) * CODE_W]
             )
 
-    c_cp, y_cp, z_cp, a_cp, ac_cp = {}, {}, {}, {}, {}
+    c_cp, y_cp, z_cp, a_cp = {}, {}, {}, {}
 
     def code(i):
         (e_down if i % 2 == 0 else e_up)[i].wait_recv()
@@ -368,20 +436,26 @@
         else:
             ga[...] += grown
 
+    def y_block(i, k):
+        return y_sum.at[i, pl.ds(pl.multiple_of(((y + k) % NY) * PAIR, PAIR), PAIR)]
+
     def code_y(i):
         c_cp[i].wait_recv()
         y_sum[i] = (c_own[i].astype(F32) + c_recv[i].astype(F32)).astype(BF)
-        for k in STEPS:
-            rows = pl.ds(pl.multiple_of(((y + k) % NY) * PAIR, PAIR), PAIR)
-            y_cp[i, k] = send(y_sum.at[i, rows], y_recv.at[i, k - 1], to_y(k))
+        step = 1 if i % 2 == 0 else 3
+        y_cp[i, "via"] = send(y_block(i, 2), y_via.at[i], to_y(step))
+        y_cp[i, "near"] = send(y_block(i, 4 - step), y_near.at[i], to_y(4 - step))
+
+    def code_mid(i):
+        step = 1 if i % 2 == 0 else 3
+        y_cp[i, "via"].wait_recv()
+        y_mid[i] = (y_block(i, step)[...].astype(F32) + y_via[i].astype(F32)).astype(BF)
+        y_cp[i, "far"] = send(y_mid.at[i], y_far.at[i], to_y(step))
 
     def code_z(i):
-        for k in STEPS:
-            y_cp[i, k].wait_recv()
-        rows = pl.ds(pl.multiple_of(y * PAIR, PAIR), PAIR)
-        total = y_sum[i, rows].astype(F32)
-        for k in range(3):
-            total += y_recv[i, k].astype(F32)
+        y_cp[i, "near"].wait_recv()
+        y_cp[i, "far"].wait_recv()
+        total = y_block(i, 0)[...].astype(F32) + y_near[i].astype(F32) + y_far[i].astype(F32)
         z_sum[i] = total.astype(BF)
         z_cp[i] = send(z_sum.at[i], z_recv.at[i], to_zh)
 
@@ -392,19 +466,41 @@
         z_cp[i].wait_recv()
         at = ag_at(zls[i], y)
         at[...] = (z_sum[i].astype(F32) + z_recv[i].astype(F32)).astype(BF)
-        for k in STEPS:
-            a_cp[i, k] = send(at, at, to_y(k))
-        ac_cp[i, 0] = send(at, at, to_c)
+        a_cp[i, "up"] = send(at, at, to_y(1))
+        a_cp[i, "down"] = send(at, at, to_y(3))
+        send(at, at, to_c, "ag")
 
     def code_out(i):
-        for k in STEPS:
-            a_cp[i, k].wait_recv()
-            at = ag_at(zls[i], (y - k + NY) % NY)
-            ac_cp[i, k] = send(at, at, to_c)
-
-    def code_done(i):
-        for k in (0,) + STEPS:
-            ac_cp[i, k].wait_recv()
+        for name, k in (("up", 3), ("down", 1)):
+            a_cp[i, name].wait_recv()
+            at = ag_at(zls[i], (y + k) % NY)
+            if name == ("up", "down")[i % 2]:
+                a_cp[i, "far"] = send(at, at, to_y(4 - k))
+            send(at, at, to_c, "ag")
+
+    def code_far(i):
+        a_cp[i, "far"].wait_recv()
+        at = ag_at(zls[i], (y + 2) % NY)
+        send(at, at, to_c, "ag")
+
+    def code_done():
+        sems.arrived(ag.at[:, :HALF], "ag", to_c)
+
+    def res_done():
+        sems.arrived(resid_ref.at[:HALF], "res", to_c)
+
+    def sends_done():
+        for goes, *rest in line:
+
+            @pl.when(goes)
+            def _():
+                line_copy(*rest).wait_send()
+
+        for i in range(NZL):
+            if G_ORDER[i]:
+                grad_copy(i, gz_recv.at[0], 0, to_zl(1)).wait_send()
+        for made in sems.started[-N_SEND:]:
+            made.wait_send()
 
     def weight_z(i):
         at = ew_at(zls[i], x)
@@ -412,7 +508,8 @@
         line_start(*line[1 + i])
         weight_x(i)
 
-    res_first(0, 0)
+    for p in range(PIECES):
+        res_first(0, p)
     attention_forward()
     weight_x2(0)
     weight_z(1)
@@ -422,75 +519,81 @@
     cotangent_y()
     weight_z(3)
     res_z(0)
-    res_first(0, 1)
     code_y(0)
+    weight_x2(2)
+    res_z(1)
+    cotangent_relay()
     res_second(0, 0)
+    res_second(0, 1)
     res_cores(0, 0)
-    weight_x2(2)
+    code_mid(0)
     code(1)
+    code_y(1)
+    weight_x2(3)
+    res_second(0, 2)
+    res_z(2)
+    code(2)
     cotangent_c()
-    res_z(1)
     grad_start(0)
-    code_y(1)
+    grad_start(1)
+    code_mid(1)
+    code_y(2)
+    res_first(1, 0)
     code_z(0)
-    weight_x2(3)
-    code(2)
-    code_y(2)
+    res_z(3)
+    code(3)
+    code_y(3)
+    res_second(0, 3)
+    res_cores(0, 1)
+    grad_start(2)
+    code_z(1)
+    code_mid(2)
+    res_first(1, 1)
+    grad_on(0)
+    grad_start(3)
     grad_attn(0)
     grad_attn(1)
     grad_attn(2)
-    code(3)
-    grad_start(1)
-    code_y(3)
-    grad_on(0)
-    grad_start(2)
-    grad_start(3)
-    code_z(1)
-    res_second(0, 1)
-    res_cores(0, 1)
+    grad_attn(3)
+    code_mid(3)
+    grad_on(1)
+    code_back(0)
     code_z(2)
-    res_first(1, 0)
-    code_back(0)
-    grad_on(1)
-    grad_attn(3)
     attention_backward()
+    grad_on(2)
     code_z(3)
+    res_first(1, 2)
     grad_z(0)
-    grad_on(2)
+    grad_on(3)
     code_back(1)
     code_out(0)
-    res_first(1, 1)
     grad_z(1)
-    grad_on(3)
+    res_second(1, 0)
+    res_second(1, 1)
+    res_first(1, 3)
     code_back(2)
-    res_second(1, 0)
+    grad_z(3)
+    code_out(1)
+    code_back(3)
     res_cores(1, 0)
-    code_out(1)
+    res_second(1, 2)
     grad_z(2)
-    grad_z(3)
-    code_back(3)
+    code_out(2)
+    code_far(0)
+    code_far(1)
     res_last(0, 0)
     res_last(0, 1)
-    code_out(2)
-    res_second(1, 1)
+    code_out(3)
+    res_second(1, 3)
+    code_far(2)
     res_cores(1, 1)
-    code_out(3)
-    for i in range(NZL):
-        code_done(i)
+    res_last(1, 0)
+    code_far(3)
     grad_end()
-    res_last(1, 0)
     res_last(1, 1)
-
-    for made in res_c:
-        made.wait_recv()
-    for goes, *rest in line:
-
-        @pl.when(goes)
-        def _():
-            line_copy(*rest).wait_send()
-
-    for made in sems.started:
-        made.wait_send()
+    code_done()
+    res_done()
+    sends_done()
 
 
 STEP_BLOCKS = 8
@@ -498,11 +601,9 @@
 
 
 def close_kernel(
-    resid_ref, cs_ref, dec_hbm, dq_in, dk_in, dv_in, gw_in,
-    out_ref, dq_ref, dk_ref, dv_ref, gw_ref, dec_ref, layer, copy_sem, out_sem,
+    resid_ref, cs_ref, dec_ref, dq_in, dk_in, dv_in, gw_in,
+    out_ref, dq_ref, dk_ref, dv_ref, gw_ref, layer, copy_sem, out_sem,
 ):
-    load = pltpu.make_async_copy(dec_hbm, dec_ref, copy_sem.at[4])
-    load.start()
     copies = [
         pltpu.make_async_copy(src, dst, copy_sem.at[i])
         for i, (src, dst) in enumerate(
@@ -511,7 +612,6 @@
     ]
     for copy in copies:
         copy.start()
-    load.wait()
     depth, width = STEP_BLOCKS * CODE_W, STEP_BLOCKS * BLOCK
     per = CLOSE_STEPS // NZL
     row = lax.broadcasted_iota(jnp.int32, (depth, BLOCK), 0) // CODE_W
@@ -543,8 +643,7 @@
     dec_rows = decoder.reshape(CODE, BLOCK)
     operands = (queries, key_rows, value_rows, residual_in, out_weight, encoder, dec_rows, grad_out)
     operands = [pltpu.with_memory_space_constraint(a, pltpu.HBM) for a in operands]
-    dec_rows = operands[6]
-    resid, code_sum, dq, dk, dv, gw = pl.pallas_call(
+    resid, code_sum, dq, dk, dv, gw, dec_rows = pl.pallas_call(
         main_kernel,
         out_shape=(
             pltpu.VMEM((SEQ, D), BF),
@@ -553,16 +652,16 @@
             pltpu.VMEM((SEQ, AW), BF),
             pltpu.VMEM((SEQ, AW), BF),
             pltpu.VMEM((OWN * BLOCK, AW), F32),
+            pltpu.VMEM((CODE, BLOCK), BF),
         ),
         in_specs=[anywhere] * 8,
-        out_specs=(vmem,) * 6,
+        out_specs=(vmem,) * 7,
         scratch_shapes=[
             pltpu.VMEM((SEQ, AW), BF),
             pltpu.VMEM((SEQ, AW), BF),
             pltpu.VMEM((SEQ, AW), BF),
             pltpu.VMEM((OWN * BLOCK, AW), BF),
             pltpu.VMEM((OWN, CODE_W, BLOCK), BF),
-            pltpu.VMEM((CODE, BLOCK), BF),
             pltpu.VMEM((TB, D), BF),
             pltpu.VMEM((NZL, CH, AW), BF),
             pltpu.VMEM((NZL, SEQ, CH), BF),
@@ -573,7 +672,10 @@
             pltpu.VMEM((4, HALF, CH), BF),
             pltpu.VMEM((4, HALF, CH), BF),
             pltpu.VMEM((4, HALF, CH), BF),
-            pltpu.VMEM((4, 3, PAIR, CH), BF),
+            pltpu.VMEM((4, PAIR, CH), BF),
+            pltpu.VMEM((4, PAIR, CH), BF),
+            pltpu.VMEM((4, PAIR, CH), BF),
+            pltpu.VMEM((4, PAIR, CH), BF),
             pltpu.VMEM((4, PAIR, CH), BF),
             pltpu.VMEM((4, PAIR, CH), BF),
             pltpu.VMEM((NZL, NX, ER, AW), BF),
@@ -583,9 +685,12 @@
             pltpu.VMEM((NZL, ER, AW), BF),
             pltpu.VMEM((NZL, ER, AW), BF),
             pltpu.VMEM((3, ER, AW), BF),
-            pltpu.SemaphoreType.DMA((N_SEMS,)),
-            pltpu.SemaphoreType.DMA((N_SEMS,)),
+            pltpu.VMEM((ER, AW), BF),
+            pltpu.SemaphoreType.DMA((N_SEND,)),
+            pltpu.SemaphoreType.DMA((N_RECV,)),
             pltpu.SemaphoreType.DMA((5,)),
+            pltpu.SemaphoreType.DMA((NZL,)),
+            pltpu.SemaphoreType.DMA((NZL,)),
             pltpu.SemaphoreType.DMA((NZL,)),
             pltpu.SemaphoreType.DMA((8,)),
         ],
@@ -604,12 +709,11 @@
             pltpu.HBM((SEQ, AW), BF),
             pltpu.HBM((OWN * BLOCK, AW), F32),
         ),
-        in_specs=[vmem, vmem, anywhere, vmem, vmem, vmem, vmem],
+        in_specs=[vmem] * 7,
         out_specs=(anywhere,) * 5,
         scratch_shapes=[
-            pltpu.VMEM((CODE, BLOCK), BF),
             pltpu.VMEM((SEQ, D), BF),
-            pltpu.SemaphoreType.DMA((5,)),
+            pltpu.SemaphoreType.DMA((4,)),
             pltpu.SemaphoreType.DMA((CLOSE_STEPS,)),
         ],
         name="close",

time: 85.2 us -> 77.1 us (0.905)
  Pallas kernels: 84.4 us -> 76.4 us
    pallas_call x1, Pallas kernels: 79.6 us -> 72.7 us  [local(): pl.pallas_call(main_kernel, out_shape=(pltpu.VMEM((SEQ, D), BF), pltpu.VM...]
    pallas_call x1, Pallas kernels: 4.79 us -> 3.63 us  [local(): pl.pallas_call(close_kernel, out_shape=(pltpu.HBM((SEQ, D), BF), pltpu.HB...]
where the time goes in v4:
time: 77.1 us; the launch traced here: 77 us
  Pallas kernels  76.4 us (99%)
    pallas_call x1, Pallas kernels, local(): pl.pallas_call(main_kernel, out_shape=(pltpu.VMEM((SEQ, D), BF), pltpu.VM...  72.7 us
    pallas_call x1, Pallas kernels, local(): pl.pallas_call(close_kernel, out_shape=(pltpu.HBM((SEQ, D), BF), pltpu.HB...  3.63 us

profile of v4, /device:TPU:1, one launch (start us, length us, event | category | flops | bytes accessed | tf_op | source)
XLA Modules:
  0.0 77.0 jit_solution(17403589869674757374)
XLA Ops:
  0.6 72.7 %exchange.1 = (bf16[256,12288]{1,0:T(8,128)(2,1)S(1)}, bf16[4,256,768]{2,1,0:T(8,128)(2,1)S(1)}, bf16[256,384]{1,0:T(8,128)(2,1)S(1)}, bf16[256,384]{1,0:T(8,128...) custom-call(bf16[256,384]{1,0:T(8,128)(2,1)} %q_hbm.1, ...), custom_call_target="tpu_custom_call" | custom-call | tf_op jit(solution)/shard_map/exchange/pallas_call | solution.py:646
  73.4 3.6 %close.1 = (bf16[256,12288]{1,0:T(8,128)(2,1)}, bf16[256,384]{1,0:T(8,128)(2,1)}, bf16[256,384]{1,0:T(8,128)(2,1)}, bf16[256,384]{1,0:T(8,128)(2,1)}, f32[768,384]{1,0:T(8,128)}) custom-call(bf16[256,12288]{1,0:T(8,128)(2,1)S(1)} %get-tuple-element.12.resid_ref, bf16[4,256,768]{2,1,0:T(8,128)(2,1)S(1)} %get-tuple-element.13.cs_ref, ...), custom_call_target="tpu_custom_call" | custom-call | tf_op jit(solution)/shard_map/close/pallas_call | solution.py:703

commit v5 on v4

--- a/solution.py
+++ b/solution.py
@@ -43,7 +43,7 @@
     return ((t % NC) * NY + t // (NC * NZH)) * NZH + (t // NC) % NZH
 
 
-N_SEND, N_RECV = 48, 96
+N_SEND, N_RECV = 48, 94
 
 
 class Sems:
@@ -178,6 +178,8 @@
     for entry in line[:2]:
         line_start(*entry)
     e_up, e_down, e_far = {}, {}, {}
+    inner = jnp.logical_and(zl > 0, zl < NZL - 1)
+    outer = jnp.logical_not(inner)
 
     def weight_x(i):
         e_up[i] = send(ew_at(zls[i], x), ew_at(zls[i], x), to_x(1))
@@ -265,9 +267,10 @@
         at = res_at(y_, shards[i], p)
         res[name, i, p] = send(at, at, target)
 
-    def res_core(y_, i, half):
-        rows = pl.ds(pl.multiple_of((y_ * NZH + shards[i]) * (NC * TB) + c * TB, TB), TB)
-        at = resid_ref.at[rows, half * (D // 2) : (half + 1) * (D // 2)]
+    def res_core(k, i, p, count=1):
+        rows = ((y + k) % NY * NZH + shards[i]) * (NC * TB) + c * TB
+        width = D // PIECES
+        at = resid_ref.at[pl.ds(pl.multiple_of(rows, TB), TB), p * width : (p + count) * width]
         send(at, at, to_c, "res")
 
     def res_z(p):
@@ -287,15 +290,14 @@
         if p % 2:
             res_move("far", (y + 1) % NY, i, p, to_y(3))
 
-    def res_cores(i, half):
-        res_core(y, i, half)
-        res_core((y + 3) % NY, i, half)
-        res_core((y + 1) % NY, i, half)
-
-    def res_last(i, half):
-        for p in (2 * half, 2 * half + 1):
-            res["far", i, p].wait_recv()
-        res_core((y + 2) % NY, i, half)
+    def res_cores(i, p, count=1):
+        res_core(3, i, p, count)
+        res_core(1, i, p, count)
+
+    def res_last(i, p, count=1):
+        for q in range(p, p + count):
+            res["far", i, q].wait_recv()
+        res_core(2, i, p, count)
 
     scale = 1.0 / math.sqrt(HD)
 
@@ -377,7 +379,6 @@
             def _():
                 grad_copy(i, gz_via, 3, ((zl + step) * NX + x, t)).start()
 
-    inner = jnp.logical_and(zl > 0, zl < NZL - 1)
 
     def grad_copy(i, dst, slot, target):
         return pltpu.make_async_remote_copy(
@@ -503,30 +504,42 @@
             made.wait_send()
 
     def weight_z(i):
+        weight_line(i)
+        weight_x(i)
+
+    def weight_line(i):
         at = ew_at(zls[i], x)
         wait_for(at, line_send.at[0], line_recv.at[zls[i]], to_zl(1))
         line_start(*line[1 + i])
-        weight_x(i)
-
-    for p in range(PIECES):
+
+    def weight_last(here):
+        @pl.when(here)
+        def _():
+            weight_line(NZL - 1)
+
+    for p in range(PIECES - 1):
         res_first(0, p)
     attention_forward()
     weight_x2(0)
     weight_z(1)
     weight_z(2)
     code(0)
+    weight_last(inner)
     weight_x2(1)
     cotangent_y()
-    weight_z(3)
+    code_y(0)
+    weight_last(outer)
+    weight_x(3)
     res_z(0)
-    code_y(0)
     weight_x2(2)
     res_z(1)
     cotangent_relay()
+    res_first(0, 3)
+    code_mid(0)
     res_second(0, 0)
     res_second(0, 1)
-    res_cores(0, 0)
-    code_mid(0)
+    res_core(0, 0, 0, 4)
+    res_cores(0, 0, 2)
     code(1)
     code_y(1)
     weight_x2(3)
@@ -544,53 +557,58 @@
     code(3)
     code_y(3)
     res_second(0, 3)
-    res_cores(0, 1)
+    res_cores(0, 2, 2)
     grad_start(2)
     code_z(1)
     code_mid(2)
     res_first(1, 1)
     grad_on(0)
+    res_core(0, 1, 0, 2)
     grad_start(3)
     grad_attn(0)
     grad_attn(1)
     grad_attn(2)
     grad_attn(3)
+    res_last(0, 0, 2)
+    res_first(1, 2)
     code_mid(3)
     grad_on(1)
     code_back(0)
     code_z(2)
     attention_backward()
     grad_on(2)
-    code_z(3)
-    res_first(1, 2)
     grad_z(0)
     grad_on(3)
+    res_first(1, 3)
+    res_core(0, 1, 2, 2)
+    code_z(3)
     code_back(1)
     code_out(0)
     grad_z(1)
     res_second(1, 0)
     res_second(1, 1)
-    res_first(1, 3)
+    res_cores(1, 0, 2)
+    res_last(0, 2, 2)
     code_back(2)
     grad_z(3)
     code_out(1)
     code_back(3)
-    res_cores(1, 0)
     res_second(1, 2)
     grad_z(2)
     code_out(2)
     code_far(0)
+    res_second(1, 3)
+    res_cores(1, 2)
+    code_out(3)
     code_far(1)
-    res_last(0, 0)
-    res_last(0, 1)
-    code_out(3)
-    res_second(1, 3)
+    res_last(1, 0)
+    res_last(1, 1)
+    res_cores(1, 3)
     code_far(2)
-    res_cores(1, 1)
-    res_last(1, 0)
     code_far(3)
+    res_last(1, 2)
     grad_end()
-    res_last(1, 1)
+    res_last(1, 3)
     code_done()
     res_done()
     sends_done()

time: 77.1 us -> 73.1 us (0.948)
  Pallas kernels: 76.4 us -> 72.3 us
    pallas_call x1, Pallas kernels: 72.7 us -> 68.7 us  [local(): pl.pallas_call(main_kernel, out_shape=(pltpu.VMEM((SEQ, D), BF), pltpu.VM...]
where the time goes in v5:
time: 73.1 us; the launch traced here: 72.9 us
  Pallas kernels  72.3 us (99%)
    pallas_call x1, Pallas kernels, local(): pl.pallas_call(main_kernel, out_shape=(pltpu.VMEM((SEQ, D), BF), pltpu.VM...  68.7 us
    pallas_call x1, Pallas kernels, local(): pl.pallas_call(close_kernel, out_shape=(pltpu.HBM((SEQ, D), BF), pltpu.HB...  3.63 us

profile of v5, /device:TPU:1, one launch (start us, length us, event | category | flops | bytes accessed | tf_op | source)
XLA Modules:
  0.0 72.9 jit_solution(4363161014600577870)
XLA Ops:
  0.6 68.7 %exchange.1 = (bf16[256,12288]{1,0:T(8,128)(2,1)S(1)}, bf16[4,256,768]{2,1,0:T(8,128)(2,1)S(1)}, bf16[256,384]{1,0:T(8,128)(2,1)S(1)}, bf16[256,384]{1,0:T(8,128...) custom-call(bf16[256,384]{1,0:T(8,128)(2,1)} %q_hbm.1, ...), custom_call_target="tpu_custom_call" | custom-call | tf_op jit(solution)/shard_map/exchange/pallas_call | solution.py:664
  69.3 3.6 %close.1 = (bf16[256,12288]{1,0:T(8,128)(2,1)}, bf16[256,384]{1,0:T(8,128)(2,1)}, bf16[256,384]{1,0:T(8,128)(2,1)}, bf16[256,384]{1,0:T(8,128)(2,1)}, f32[768,384]{1,0:T(8,128)}) custom-call(bf16[256,12288]{1,0:T(8,128)(2,1)S(1)} %get-tuple-element.12.resid_ref, bf16[4,256,768]{2,1,0:T(8,128)(2,1)S(1)} %get-tuple-element.13.cs_ref, ...), custom_call_target="tpu_custom_call" | custom-call | tf_op jit(solution)/shard_map/close/pallas_call | solution.py:721

commit v6 on v5

--- a/solution.py
+++ b/solution.py
@@ -43,7 +43,8 @@
     return ((t % NC) * NY + t // (NC * NZH)) * NZH + (t // NC) % NZH
 
 
-N_SEND, N_RECV = 48, 94
+KINDS = ("ew", "gc", "res", "grad", "code", "back")
+N_RECV = 94
 
 
 class Sems:
@@ -56,21 +57,28 @@
             self.used += 1
         return self.recv.at[self.groups[group]]
 
-    def copy(self, src, dst, target, group=None):
-        n = len(self.started)
-        if n >= N_SEND:
-            self.started[n - N_SEND].wait_send()
+    def copy(self, kind, src, dst, target, group=None):
         made = pltpu.make_async_remote_copy(
             src_ref=src,
             dst_ref=dst,
-            send_sem=self.send.at[n % N_SEND],
-            recv_sem=self.slot(n if group is None else group),
+            send_sem=self.send.at[KINDS.index(kind)],
+            recv_sem=self.slot(len(self.started) if group is None else group),
             device_id=target,
             device_id_type=MESH,
         )
         made.start()
         self.started.append(made)
         return made
+
+    def sent(self, kind, ref, target):
+        pltpu.make_async_remote_copy(
+            src_ref=ref,
+            dst_ref=ref,
+            send_sem=self.send.at[KINDS.index(kind)],
+            recv_sem=self.recv.at[0],
+            device_id=target,
+            device_id_type=MESH,
+        ).wait_send()
 
     def arrived(self, ref, group, target):
         wait_for(ref, self.send.at[0], self.slot(group), target)
@@ -182,18 +190,18 @@
     outer = jnp.logical_not(inner)
 
     def weight_x(i):
-        e_up[i] = send(ew_at(zls[i], x), ew_at(zls[i], x), to_x(1))
-        e_down[i] = send(ew_at(zls[i], x), ew_at(zls[i], x), to_x(3))
+        e_up[i] = send("ew", ew_at(zls[i], x), ew_at(zls[i], x), to_x(1))
+        e_down[i] = send("ew", ew_at(zls[i], x), ew_at(zls[i], x), to_x(3))
 
     def weight_x2(i):
         if i % 2 == 0:
             e_up[i].wait_recv()
             at = ew_at(zls[i], (x + 3) % NX)
-            e_far[i] = send(at, at, to_x(1))
+            e_far[i] = send("ew", at, at, to_x(1))
         else:
             e_down[i].wait_recv()
             at = ew_at(zls[i], (x + 1) % NX)
-            e_far[i] = send(at, at, to_x(3))
+            e_far[i] = send("ew", at, at, to_x(3))
 
     weight_x(0)
 
@@ -220,16 +228,16 @@
         gcb[g // 6, mine, (g % 6) * BLOCK : (g % 6 + 1) * BLOCK] = picked.astype(BF)
 
     gc_up, gc_down, gc_far = {}, {}, {}
-    gc_z = send(gcb.at[:, mine], gcb.at[:, mine], to_zh)
+    gc_z = send("gc", gcb.at[:, mine], gcb.at[:, mine], to_zh)
 
     def cotangent_first(i):
         at = gcb.at[:, (mine, other)[i]]
-        gc_up[i] = send(at, at, to_y(1))
-        gc_down[i] = send(at, at, to_y(3))
+        gc_up[i] = send("gc", at, at, to_y(1))
+        gc_down[i] = send("gc", at, at, to_y(3))
 
     def cotangent_core(y_):
         at = gcb.at[:, block_rows(place_of(y_, 0, c), NZH)]
-        send(at, at, to_c, "gc")
+        send("gc", at, at, to_c, "gc")
 
     def cotangent_y():
         gc_z.wait_recv()
@@ -239,11 +247,11 @@
     def cotangent_relay():
         gc_up[0].wait_recv()
         at = gcb.at[:, block_rows(place_of((y + 3) % NY, zh, c))]
-        gc_far[0] = send(at, at, to_y(1))
+        gc_far[0] = send("gc", at, at, to_y(1))
         gc_down[0].wait_recv()
         gc_down[1].wait_recv()
         at = gcb.at[:, block_rows(place_of((y + 1) % NY, 1 - zh, c))]
-        gc_far[1] = send(at, at, to_y(3))
+        gc_far[1] = send("gc", at, at, to_y(3))
         cotangent_core((y + 1) % NY)
         gc_up[1].wait_recv()
         cotangent_core((y + 3) % NY)
@@ -265,13 +273,13 @@
 
     def res_move(name, y_, i, p, target):
         at = res_at(y_, shards[i], p)
-        res[name, i, p] = send(at, at, target)
+        res[name, i, p] = send("res", at, at, target)
 
     def res_core(k, i, p, count=1):
         rows = ((y + k) % NY * NZH + shards[i]) * (NC * TB) + c * TB
         width = D // PIECES
         at = resid_ref.at[pl.ds(pl.multiple_of(rows, TB), TB), p * width : (p + count) * width]
-        send(at, at, to_c, "res")
+        send("res", at, at, to_c, "res")
 
     def res_z(p):
         res_move("z", y, 0, p, to_zh)
@@ -343,17 +351,17 @@
             gp[i, x_] = term[x_ * ER : (x_ + 1) * ER].astype(BF)
         far = gp.at[i, (x + 2) % NX]
         if i % 2 == 0:
-            g_up[i] = send(far, g_via.at[i], to_x(1))
-            g_down[i] = send(gp.at[i, (x + 3) % NX], g_near.at[i], to_x(3))
+            g_up[i] = send("grad", far, g_via.at[i], to_x(1))
+            g_down[i] = send("grad", gp.at[i, (x + 3) % NX], g_near.at[i], to_x(3))
         else:
-            g_down[i] = send(far, g_via.at[i], to_x(3))
-            g_up[i] = send(gp.at[i, (x + 1) % NX], g_near.at[i], to_x(1))
+            g_down[i] = send("grad", far, g_via.at[i], to_x(3))
+            g_up[i] = send("grad", gp.at[i, (x + 1) % NX], g_near.at[i], to_x(1))
 
     def grad_on(i):
         step = 1 if i % 2 == 0 else 3
         (g_up if i % 2 == 0 else g_down)[i].wait_recv()
         g_mid[i] = (gp[i, (x + step) % NX].astype(F32) + g_via[i].astype(F32)).astype(BF)
-        g_on[i] = send(g_mid.at[i], g_far.at[i], to_x(step))
+        g_on[i] = send("grad", g_mid.at[i], g_far.at[i], to_x(step))
 
     def grad_z(i):
         (g_down if i % 2 == 0 else g_up)[i].wait_recv()
@@ -428,7 +436,7 @@
             def _():
                 c_send[i] = part
 
-        c_cp[i] = send(c_send.at[i], c_recv.at[i], to_c)
+        c_cp[i] = send("code", c_send.at[i], c_recv.at[i], to_c)
 
     def grad_attn(i):
         grown = nn(gcb[zls[i]], ew[zls[i]])
@@ -444,21 +452,21 @@
         c_cp[i].wait_recv()
         y_sum[i] = (c_own[i].astype(F32) + c_recv[i].astype(F32)).astype(BF)
         step = 1 if i % 2 == 0 else 3
-        y_cp[i, "via"] = send(y_block(i, 2), y_via.at[i], to_y(step))
-        y_cp[i, "near"] = send(y_block(i, 4 - step), y_near.at[i], to_y(4 - step))
+        y_cp[i, "via"] = send("code", y_block(i, 2), y_via.at[i], to_y(step))
+        y_cp[i, "near"] = send("code", y_block(i, 4 - step), y_near.at[i], to_y(4 - step))
 
     def code_mid(i):
         step = 1 if i % 2 == 0 else 3
         y_cp[i, "via"].wait_recv()
         y_mid[i] = (y_block(i, step)[...].astype(F32) + y_via[i].astype(F32)).astype(BF)
-        y_cp[i, "far"] = send(y_mid.at[i], y_far.at[i], to_y(step))
+        y_cp[i, "far"] = send("code", y_mid.at[i], y_far.at[i], to_y(step))
 
     def code_z(i):
         y_cp[i, "near"].wait_recv()
         y_cp[i, "far"].wait_recv()
         total = y_block(i, 0)[...].astype(F32) + y_near[i].astype(F32) + y_far[i].astype(F32)
         z_sum[i] = total.astype(BF)
-        z_cp[i] = send(z_sum.at[i], z_recv.at[i], to_zh)
+        z_cp[i] = send("code", z_sum.at[i], z_recv.at[i], to_zh)
 
     def ag_at(z_, y_):
         return ag.at[z_, pl.ds(pl.multiple_of((c * NY + y_) * PAIR, PAIR), PAIR)]
@@ -467,22 +475,22 @@
         z_cp[i].wait_recv()
         at = ag_at(zls[i], y)
         at[...] = (z_sum[i].astype(F32) + z_recv[i].astype(F32)).astype(BF)
-        a_cp[i, "up"] = send(at, at, to_y(1))
-        a_cp[i, "down"] = send(at, at, to_y(3))
-        send(at, at, to_c, "ag")
+        a_cp[i, "up"] = send("back", at, at, to_y(1))
+        a_cp[i, "down"] = send("back", at, at, to_y(3))
+        send("back", at, at, to_c, "ag")
 
     def code_out(i):
         for name, k in (("up", 3), ("down", 1)):
             a_cp[i, name].wait_recv()
             at = ag_at(zls[i], (y + k) % NY)
             if name == ("up", "down")[i % 2]:
-                a_cp[i, "far"] = send(at, at, to_y(4 - k))
-            send(at, at, to_c, "ag")
+                a_cp[i, "far"] = send("back", at, at, to_y(4 - k))
+            send("back", at, at, to_c, "ag")
 
     def code_far(i):
         a_cp[i, "far"].wait_recv()
         at = ag_at(zls[i], (y + 2) % NY)
-        send(at, at, to_c, "ag")
+        send("back", at, at, to_c, "ag")
 
     def code_done():
         sems.arrived(ag.at[:, :HALF], "ag", to_c)
@@ -500,8 +508,12 @@
         for i in range(NZL):
             if G_ORDER[i]:
                 grad_copy(i, gz_recv.at[0], 0, to_zl(1)).wait_send()
-        for made in sems.started[-N_SEND:]:
-            made.wait_send()
+        sems.sent("ew", ew.at[:3], to_c)
+        sems.sent("gc", gcb.at[:, : SEQ - TB], to_c)
+        sems.sent("res", resid_ref.at[: SEQ - TB], to_c)
+        sems.sent("grad", gp.at[:3], to_c)
+        sems.sent("code", ag, to_c)
+        sems.sent("back", ag.at[:, : SEQ - PAIR], to_c)
 
     def weight_z(i):
         weight_line(i)
@@ -704,7 +716,7 @@
             pltpu.VMEM((NZL, ER, AW), BF),
             pltpu.VMEM((3, ER, AW), BF),
             pltpu.VMEM((ER, AW), BF),
-            pltpu.SemaphoreType.DMA((N_SEND,)),
+            pltpu.SemaphoreType.DMA((len(KINDS),)),
             pltpu.SemaphoreType.DMA((N_RECV,)),
             pltpu.SemaphoreType.DMA((5,)),
             pltpu.SemaphoreType.DMA((NZL,)),

time: 73.1 us -> 72.7 us (level)
  no operation moved by 1% of the time
where the time goes in v6:
time: 72.7 us; the launch traced here: 72.6 us
  Pallas kernels  71.9 us (99%)
    pallas_call x1, Pallas kernels, local(): pl.pallas_call(main_kernel, out_shape=(pltpu.VMEM((SEQ, D), BF), pltpu.VM...  68.3 us
    pallas_call x1, Pallas kernels, local(): pl.pallas_call(close_kernel, out_shape=(pltpu.HBM((SEQ, D), BF), pltpu.HB...  3.63 us

profile of v6, /device:TPU:1, one launch (start us, length us, event | category | flops | bytes accessed | tf_op | source)
XLA Modules:
  0.0 72.6 jit_solution(6819068495068768271)
XLA Ops:
  0.6 68.3 %exchange.1 = (bf16[256,12288]{1,0:T(8,128)(2,1)S(1)}, bf16[4,256,768]{2,1,0:T(8,128)(2,1)S(1)}, bf16[256,384]{1,0:T(8,128)(2,1)S(1)}, bf16[256,384]{1,0:T(8,128...) custom-call(bf16[256,384]{1,0:T(8,128)(2,1)} %q_hbm.1, ...), custom_call_target="tpu_custom_call" | custom-call | tf_op jit(solution)/shard_map/exchange/pallas_call | solution.py:676
  69.0 3.6 %close.1 = (bf16[256,12288]{1,0:T(8,128)(2,1)}, bf16[256,384]{1,0:T(8,128)(2,1)}, bf16[256,384]{1,0:T(8,128)(2,1)}, bf16[256,384]{1,0:T(8,128)(2,1)}, f32[768,384]{1,0:T(8,128)}) custom-call(bf16[256,12288]{1,0:T(8,128)(2,1)S(1)} %get-tuple-element.12.resid_ref, bf16[4,256,768]{2,1,0:T(8,128)(2,1)S(1)} %get-tuple-element.13.cs_ref, ...), custom_call_target="tpu_custom_call" | custom-call | tf_op jit(solution)/shard_map/close/pallas_call | solution.py:733
